TPU v7x, 32 devices: a whole 2x2x4 slice. The times are simulated.
32 devices in a mesh: groups: 2 (over y), freq: 4 (over z), read: 2 (over x), pair: 2 (over core).
Axes of the slice: x: 2, y: 2, z: 4, core: 2. Of those that a mesh axis runs over, the one named last changes fastest.
Arguments:
- exposures: float32 [8, 2048, 2048], P(('groups', 'read', 'pair'), 'freq'), parts along dimension 0, may hold values from -6 to 6
- stamps: float32 [8, 16, 16], P('groups'), parts along dimension 0, may hold values from -1 to 1, as said below
- zero_point: float32 [8], P('groups'), parts along dimension 0, may hold values from 0.5 to 2
- noise_var: float32 [8], P('groups'), parts along dimension 0, may hold values from 0.25 to 4
- footprint: int32 [8, 2], P('groups'), parts along dimension 0, may hold values from 0 to 2048, as said below
- accept: int32 [8], P('groups'), parts along dimension 0, may hold values from 0 to 1, as said below
- assign: int32 [8], P('groups'), parts along dimension 0, may hold values from 0 to 3, each once
Outputs:
- coadd: float32 [2, 4096, 1024], P(None, ('groups', 'read', 'pair'), 'freq'), parts along dimension 1
There are 2 independent parts, one for each index of `groups`. A program takes and returns all parts, laid end to end along the dimension named above; each array names one. Nothing has to cross between parts.
Inputs may be any that keep to these rules, and one draw needn't show every extreme that they name: `stamps`: each stamp is 1 at row 8 and column 8, and the absolute values of its other entries sum to at most 0.9. For every exposure footprint[e, 0] < footprint[e, 1] and the two differ by at least 512; some exposure covers all 2048 rows. `accept`: at least one exposure is rejected, and at least one exposure that covers all 2048 rows is accepted. `assign`: each exposure sits in exactly one slot.
All inputs are finite; a program needn't handle non-finite values.
Results may differ from a plain program's by a relative error of at most 0.0001.
Values sent between devices are 32-bit elements; how exact they have to be, the bound alone decides.
A program may use at most 64 MiB of HBM per device.

v0:
```python
import functools
import math

import jax
import jax.numpy as jnp
import ml_dtypes
import numpy as np
from jax import lax
from jax.experimental import pallas as pl
from jax.experimental.pallas import tpu as pltpu
from jax.sharding import PartitionSpec as P

HIGHEST = lax.Precision.HIGHEST
TWO_PI = 2.0 * math.pi
HALO = 16
TILE = 128
BF16 = jnp.bfloat16
F32 = jnp.float32
READERS = ("read", "pair")


def split_np(table):
    hi = table.astype(np.float32).astype(ml_dtypes.bfloat16)
    lo = (table - hi.astype(np.float64)).astype(np.float32).astype(ml_dtypes.bfloat16)
    return hi, lo


def split(value):
    hi = value.astype(BF16)
    return hi, (value - hi.astype(F32)).astype(BF16)


def angles(left, right, modulus):
    return (np.outer(left, right) % modulus).astype(np.float64) * (TWO_PI / modulus)


def dot(left, right):
    return jnp.dot(left, right, preferred_element_type=F32)


def column_order(width, freqs, readers):
    share = width // 2 // freqs // readers
    parity = np.arange(2)[:, None, None, None]
    reader = np.arange(readers)[None, :, None, None]
    freq = np.arange(freqs)[None, None, :, None]
    inner = np.arange(share // 2)[None, None, None, :]
    ids = freq * (share * readers) + reader * share + 2 * inner + parity
    return ids.reshape(2, -1, TILE)


def row_tables(ids, width):
    half = np.arange(width // 2)
    parts = []
    for tile in range(ids.shape[1]):
        both = []
        for parity in range(2):
            phase = angles(half, ids[parity, tile], width)
            both.append(np.concatenate([np.cos(phase), -np.sin(phase)], axis=1))
        parts.append(np.stack(both))
    return split_np(np.stack(parts))


def front_kernel(info, low, block, high, taps, th, tl, out, ext, ch, cl, grid):
    rows, width = block.shape
    half = width // 2
    height = info[3]

    @pl.when(pl.program_id(0) == 0)
    def _():
        ext[:HALO] = low[...]
        ext[HALO : HALO + rows] = block[...]
        ext[HALO + rows :] = high[...]
        cols = lax.broadcasted_iota(jnp.int32, (16, width), 1)

        def clean(i, carry):
            at = pl.multiple_of(i * 16, 16)
            piece = ext[pl.ds(at, 32), :]
            mid = piece[8:24]
            ids = info[0] - 8 + at + lax.broadcasted_iota(jnp.int32, (16, 1), 0)
            ids = jnp.where(ids < 0, ids + height, ids)
            ids = jnp.where(ids >= height, ids - height, ids)
            up = jnp.where(ids == 0, 0.0, piece[7:23])
            down = jnp.where(ids == height - 1, 0.0, piece[9:25])
            left = jnp.where(cols == 0, 0.0, pltpu.roll(mid, 1, 1))
            right = jnp.where(cols == width - 1, 0.0, pltpu.roll(mid, width - 1, 1))
            inside = (ids >= info[1]) & (ids < info[2])
            cell = jnp.where(inside, mid - 0.25 * (up + down + left + right), 0.0)
            for parity in range(2):
                if parity == 0:
                    fold = cell[:, :half] + cell[:, half:]
                else:
                    fold = cell[:, :half] - cell[:, half:]
                hi, lo = split(fold)
                ch[parity, pl.ds(at, 16), :] = hi
                cl[parity, pl.ds(at, 16), :] = lo
            return carry

        lax.fori_loop(0, (rows + 16) // 16, clean, 0)

    for parity in range(2):
        grid[parity] = (
            dot(ch[parity], th[0, parity])
            + dot(ch[parity], tl[0, parity])
            + dot(cl[parity], th[0, parity])
        )

    def fir(i, carry):
        at = pl.multiple_of(i * 32, 32)
        for parity in range(2):
            re = grid[parity, pl.ds(at, 48), :TILE]
            im = grid[parity, pl.ds(at, 48), TILE:]
            sum_re = jnp.zeros((32, TILE), F32)
            sum_im = jnp.zeros((32, TILE), F32)
            for k in range(8):
                shift_re = re[k : k + 40]
                shift_im = im[k : k + 40]
                for a in (k, k + 8):
                    qr = taps[0, parity, 0, a : a + 1, :]
                    qi = taps[0, parity, 1, a : a + 1, :]
                    xr = shift_re[a - k : a - k + 32]
                    xi = shift_im[a - k : a - k + 32]
                    sum_re = sum_re + (qr * xr + qi * xi)
                    sum_im = sum_im + (qr * xi - qi * xr)
            lane = parity * 2 * TILE
            out[0, pl.ds(at, 32), lane : lane + TILE] = sum_re
            out[0, pl.ds(at, 32), lane + TILE : lane + 2 * TILE] = sum_im
        return carry

    lax.fori_loop(0, rows // 32, fir, 0)


def front(info, low, block, high, taps, tables):
    rows, width = block.shape
    tiles = tables[0].shape[0]
    whole = lambda shape: pl.BlockSpec(shape, lambda t: (0,) * len(shape))
    table_spec = pl.BlockSpec((1, 2, width // 2, 2 * TILE), lambda t: (t, 0, 0, 0))
    return pl.pallas_call(
        front_kernel,
        grid=(tiles,),
        out_shape=jax.ShapeDtypeStruct((tiles, rows, 4 * TILE), F32),
        in_specs=[
            pl.BlockSpec(memory_space=pltpu.SMEM),
            whole((HALO, width)),
            whole((rows, width)),
            whole((HALO, width)),
            pl.BlockSpec((1, 2, 2, taps.shape[3], TILE), lambda t: (t, 0, 0, 0, 0)),
            table_spec,
            table_spec,
        ],
        out_specs=pl.BlockSpec((1, rows, 4 * TILE), lambda t: (t, 0, 0)),
        scratch_shapes=[
            pltpu.VMEM((rows + 2 * HALO, width), F32),
            pltpu.VMEM((2, rows + 16, width // 2), BF16),
            pltpu.VMEM((2, rows + 16, width // 2), BF16),
            pltpu.VMEM((2, rows + 16, 2 * TILE), F32),
        ],
        compiler_params=pltpu.CompilerParams(vmem_limit_bytes=48 * 1024 * 1024),
        name="front",
    )(info, low, block, high, taps, *tables)


CHUNKS = 4
MESH = pl.DeviceIdType.MESH


def clean_rows(info, low, block, high, ext, ch, cl, height):
    rows, width = block.shape
    half = width // 2
    ext[:HALO] = low[...]
    ext[HALO : HALO + rows] = block[...]
    ext[HALO + rows :] = high[...]
    cols = lax.broadcasted_iota(jnp.int32, (16, width), 1)

    def clean(i, carry):
        at = pl.multiple_of(i * 16, 16)
        piece = ext[pl.ds(at, 32), :]
        mid = piece[8:24]
        ids = info[0] - 8 + at + lax.broadcasted_iota(jnp.int32, (16, 1), 0)
        ids = jnp.where(ids < 0, ids + height, ids)
        ids = jnp.where(ids >= height, ids - height, ids)
        up = jnp.where(ids == 0, 0.0, piece[7:23])
        down = jnp.where(ids == height - 1, 0.0, piece[9:25])
        left = jnp.where(cols == 0, 0.0, pltpu.roll(mid, 1, 1))
        right = jnp.where(cols == width - 1, 0.0, pltpu.roll(mid, width - 1, 1))
        inside = (ids >= info[1]) & (ids < info[2])
        cell = jnp.where(inside, mid - 0.25 * (up + down + left + right), 0.0)
        for parity in range(2):
            if parity == 0:
                fold = cell[:, :half] + cell[:, half:]
            else:
                fold = cell[:, :half] - cell[:, half:]
            hi, lo = split(fold)
            ch[parity, pl.ds(at, 16), :] = hi
            cl[parity, pl.ds(at, 16), :] = lo
        return carry

    lax.fori_loop(0, (rows + 16) // 16, clean, 0)


def fused_kernel(
    freqs, info, low, block, high, taps, th, tl, out,
    ext, ch, cl, grid, bufh, bufl, work, pair_in, read_in, freq_out, freq_in,
    table_sem, pair_send, pair_recv, read_send, read_recv, freq_send, freq_recv,
):
    rows, width = block.shape
    height = rows * freqs
    chunk = rows // CHUNKS
    share = TILE // freqs
    r = lax.axis_index("read")
    p = lax.axis_index("pair")
    f = lax.axis_index("freq")

    def tile_at(s):
        rd = jnp.where(s < 2, 1 - r, r)
        pd = jnp.where(s % 2 == 0, 1 - p, p)
        return rd * 2 + pd

    def table_copies(s):
        t = tile_at(s)
        return (
            pltpu.make_async_copy(th.at[t], bufh.at[s], table_sem.at[0, s]),
            pltpu.make_async_copy(tl.at[t], bufl.at[s], table_sem.at[1, s]),
        )

    def pair_copy(n):
        return pltpu.make_async_remote_copy(
            src_ref=work.at[2 * n], dst_ref=pair_in.at[n],
            send_sem=pair_send.at[n], recv_sem=pair_recv.at[n],
            device_id={"pair": 1 - p}, device_id_type=MESH,
        )

    def read_copy(c):
        part = pl.ds(c * chunk, chunk)
        return pltpu.make_async_remote_copy(
            src_ref=work.at[1, part], dst_ref=read_in.at[part],
            send_sem=read_send.at[c], recv_sem=read_recv.at[c],
            device_id={"read": 1 - r}, device_id_type=MESH,
        )

    def freq_copy(d, c):
        part = pl.ds(c * chunk, chunk)
        to = lax.rem(f + d, freqs)
        return pltpu.make_async_remote_copy(
            src_ref=freq_out.at[to, part], dst_ref=freq_in.at[f, part],
            send_sem=freq_send.at[d - 1, c], recv_sem=freq_recv.at[d - 1, c],
            device_id={"freq": to}, device_id_type=MESH,
        )

    for s in range(4):
        for copy in table_copies(s):
            copy.start()
    barrier = pltpu.get_barrier_semaphore()
    pl.semaphore_signal(barrier, inc=1, device_id={"pair": 1 - p}, device_id_type=MESH)
    pl.semaphore_signal(barrier, inc=1, device_id={"read": 1 - r}, device_id_type=MESH)
    for d in range(1, freqs):
        pl.semaphore_signal(
            barrier, inc=1, device_id={"freq": lax.rem(f + d, freqs)}, device_id_type=MESH
        )
    clean_rows(info, low, block, high, ext, ch, cl, height)
    pl.semaphore_wait(barrier, freqs + 1)

    def step(s, carry):
        for copy in table_copies(s):
            copy.wait()
        t = tile_at(s)
        for parity in range(2):
            grid[parity] = (
                dot(ch[parity], bufh[s, parity])
                + dot(ch[parity], bufl[s, parity])
                + dot(cl[parity], bufh[s, parity])
            )

        def fir(i, inner):
            at = pl.multiple_of(i * 32, 32)
            for parity in range(2):
                re = grid[parity, pl.ds(at, 48), :TILE]
                im = grid[parity, pl.ds(at, 48), TILE:]
                sum_re = jnp.zeros((32, TILE), F32)
                sum_im = jnp.zeros((32, TILE), F32)
                for k in range(8):
                    shift_re = re[k : k + 40]
                    shift_im = im[k : k + 40]
                    for a in (k, k + 8):
                        qr = taps[t, parity, 0, a : a + 1, :]
                        qi = taps[t, parity, 1, a : a + 1, :]
                        xr = shift_re[a - k : a - k + 32]
                        xi = shift_im[a - k : a - k + 32]
                        sum_re = sum_re + (qr * xr + qi * xi)
                        sum_im = sum_im + (qr * xi - qi * xr)
                lane = parity * 2 * TILE
                work[s, pl.ds(at, 32), lane : lane + TILE] = sum_re
                work[s, pl.ds(at, 32), lane + TILE : lane + 2 * TILE] = sum_im
            return inner

        lax.fori_loop(0, rows // 32, fir, 0)

        @pl.when(s == 0)
        def _():
            pair_copy(0).start()

        @pl.when(s == 1)
        def _():
            pair_copy(0).wait_recv()
            for c in range(CHUNKS):
                part = pl.ds(c * chunk, chunk)
                work[1, part, :] = work[1, part, :] + pair_in[0, part, :]
                read_copy(c).start()

        @pl.when(s == 2)
        def _():
            pair_copy(1).start()

        return carry

    lax.fori_loop(0, 4, step, 0)

    pair_copy(1).wait_recv()
    lanes = lax.broadcasted_iota(jnp.int32, (32, TILE), 1) // share
    for c in range(CHUNKS):
        read_copy(c).wait_recv()

        def pack(i, carry, c=c):
            part = pl.ds(pl.multiple_of(c * chunk + i * 32, 32), 32)
            total = work[3, part, :] + pair_in[1, part, :] + read_in[part, :]
            quads = [
                total[:, q * TILE : (q + 1) * TILE]
                for q in (0, 2, 1, 3)
            ]
            for to in range(freqs):
                result = None
                for q in range(4):
                    shift = (q - to) * share % TILE
                    moved = quads[q] if shift == 0 else pltpu.roll(quads[q], shift, 1)
                    result = moved if q == 0 else jnp.where(lanes == q, moved, result)
                freq_out[to, part, :] = result
            return carry

        lax.fori_loop(0, chunk // 32, pack, 0)
        for d in range(1, freqs):
            freq_copy(d, c).start()
    out[f] = freq_out[f]
    for n in range(2):
        pair_copy(n).wait_send()
    for c in range(CHUNKS):
        read_copy(c).wait_send()
    for d in range(1, freqs):
        for c in range(CHUNKS):
            freq_copy(d, c).wait()
        source = lax.rem(f + freqs - d, freqs)
        out[source] = freq_in[source]


def fused(info, low, block, high, taps, tables, freqs):
    rows, width = block.shape
    half = width // 2
    vmem = pl.BlockSpec(memory_space=pltpu.VMEM)
    anywhere = pl.BlockSpec(memory_space=pl.ANY)
    dma = pltpu.SemaphoreType.DMA
    return pl.pallas_call(
        functools.partial(fused_kernel, freqs),
        out_shape=jax.ShapeDtypeStruct((freqs, rows, TILE), F32),
        in_specs=[pl.BlockSpec(memory_space=pltpu.SMEM), vmem, vmem, vmem, vmem, anywhere, anywhere],
        out_specs=vmem,
        scratch_shapes=[
            pltpu.VMEM((rows + 2 * HALO, width), F32),
            pltpu.VMEM((2, rows + 16, half), BF16),
            pltpu.VMEM((2, rows + 16, half), BF16),
            pltpu.VMEM((2, rows + 16, 2 * TILE), F32),
            pltpu.VMEM((4, 2, half, 2 * TILE), BF16),
            pltpu.VMEM((4, 2, half, 2 * TILE), BF16),
            pltpu.VMEM((4, rows, 4 * TILE), F32),
            pltpu.VMEM((2, rows, 4 * TILE), F32),
            pltpu.VMEM((rows, 4 * TILE), F32),
            pltpu.VMEM((freqs, rows, TILE), F32),
            pltpu.VMEM((freqs, rows, TILE), F32),
            dma((2, 4)),
            dma((2,)),
            dma((2,)),
            dma((CHUNKS,)),
            dma((CHUNKS,)),
            dma((freqs - 1, CHUNKS)),
            dma((freqs - 1, CHUNKS)),
        ],
        compiler_params=pltpu.CompilerParams(
            collective_id=0, has_side_effects=True, vmem_limit_bytes=56 * 1024 * 1024
        ),
        cost_estimate=pl.CostEstimate(flops=7 * 10**9, bytes_accessed=14 * 2**20, transcendentals=0),
        name="fused",
    )(info, low, block, high, taps, *tables)


def column_tables(height):
    quarter = height // 4
    inner = np.arange(quarter)
    parts = []
    for j in range(4):
        phase = angles(4 * np.arange(quarter) + j, inner, height)
        parts.append(np.concatenate([np.cos(phase), np.sin(phase)], axis=1))
    return split_np(np.stack(parts))


def order_matrix(share):
    size = 2 * share
    table = np.zeros((size, 2 * size), np.float32)
    for part in range(2):
        for parity in range(2):
            for j in range(share // 2):
                source = part * share + parity * (share // 2) + j
                place = 2 * j + parity
                table[source, part * share + place] = 1.0
                table[source, size + (1 - part) * share + place] = -1.0 if part == 0 else 1.0
    return table.astype(ml_dtypes.bfloat16)


def column_kernel(x, order, th, tl, out):
    height, lanes = x.shape
    quarter = height // 4
    step = pl.program_id(0)
    for j in range(4):

        @pl.when(step == j)
        def _(j=j):
            parts = []
            for f in range(4):
                hi, lo = split(x[f * quarter : (f + 1) * quarter])
                parts.append(dot(hi, order[...]) + dot(lo, order[...]))
            if j % 2 == 0:
                even, odd = parts[0] + parts[2], parts[1] + parts[3]
                mix = even + odd if j == 0 else even - odd
                top, low = mix[:, :lanes], mix[:, lanes:]
            else:
                even, odd = parts[0] - parts[2], parts[1] - parts[3]
                sign = 1.0 if j == 1 else -1.0
                top = even[:, :lanes] + sign * odd[:, lanes:]
                low = even[:, lanes:] - sign * odd[:, :lanes]
            both = jnp.concatenate([top, low], axis=0)
            hi, lo = split(both)
            wide = dot(th[0], jnp.concatenate([hi, lo], axis=1))
            result = wide[:, :lanes] + wide[:, lanes:] + dot(tl[0], hi)
            out[pl.ds(j, quarter, stride=4), :] = result


def columns(x, order, tables):
    height, lanes = x.shape
    quarter = height // 4
    table_spec = pl.BlockSpec((1, quarter, 2 * quarter), lambda j: (j, 0, 0))
    return pl.pallas_call(
        column_kernel,
        grid=(4,),
        out_shape=jax.ShapeDtypeStruct((height, lanes), F32),
        in_specs=[
            pl.BlockSpec((height, lanes), lambda j: (0, 0)),
            pl.BlockSpec((lanes, 2 * lanes), lambda j: (0, 0)),
            table_spec,
            table_spec,
        ],
        out_specs=pl.BlockSpec((height, lanes), lambda j: (0, 0)),
        compiler_params=pltpu.CompilerParams(vmem_limit_bytes=48 * 1024 * 1024),
        name="columns",
    )(x, order, *tables)


def denom_kernel(weight, rows, cols, out):
    count = cols.shape[0]
    lanes = out.shape[1]
    total = jnp.zeros(out.shape, F32)
    rh, rl = split(rows[...])
    for e in range(count):
        chh, cll = split(cols[e])
        psf = dot(rh, chh) + dot(rh, cll) + dot(rl, chh)
        total = total + weight[e] * (psf[:, :lanes] * psf[:, :lanes] + psf[:, lanes:] * psf[:, lanes:])
    out[...] = lax.rsqrt(total)


def per_device(exposures, stamps, zero_point, noise_var, footprint, accept, assign):
    exp_dev, rows_dev, width = exposures.shape
    freqs = lax.axis_size("freq")
    readers = lax.axis_size(READERS)
    height = rows_dev * freqs
    per_freq = width // 2 // freqs
    share = per_freq // readers
    out_rows = height // readers
    stamp_len = stamps.shape[1]
    count_all = assign.shape[0]
    freq_at = lax.axis_index("freq")
    reader_at = lax.axis_index(READERS)
    ids = column_order(width, freqs, readers)
    tiles = ids.shape[1]
    offsets = np.arange(stamp_len) - stamp_len // 2

    block = exposures[0]
    forward = [(i, (i + 1) % freqs) for i in range(freqs)]
    backward = [(t, s) for s, t in forward]
    low = lax.ppermute(block[rows_dev - HALO :], "freq", forward)
    high = lax.ppermute(block[:HALO], "freq", backward)

    labels = jnp.arange(count_all, dtype=jnp.int32)
    owner = jnp.sum(jnp.where(labels == reader_at, assign, 0))
    chosen = labels == owner
    low_row = jnp.sum(jnp.where(chosen, footprint[:, 0], 0))
    high_row = jnp.sum(jnp.where(chosen, footprint[:, 1], 0))
    accepted = accept.astype(F32)
    numer_weight = accepted * zero_point / noise_var
    denom_weight = accepted * zero_point * zero_point / noise_var
    scale = 1.0 / math.sqrt(height * width)
    weight = jnp.sum(jnp.where(chosen, numer_weight, 0.0)) * scale
    stamp = jnp.sum(jnp.where(chosen[:, None, None], stamps, 0.0), axis=0) * weight
    tap_phase = angles(offsets, ids.reshape(-1), width)
    tap_table = np.stack([np.cos(tap_phase), -np.sin(tap_phase)]).astype(np.float32)
    taps = jnp.einsum("ab,cbp->cap", stamp, tap_table, precision=HIGHEST)
    taps = taps.reshape(2, stamp_len, 2, tiles, TILE).transpose(3, 2, 0, 1, 4)
    info = jnp.stack([freq_at * rows_dev, low_row, high_row, jnp.int32(height)]).astype(jnp.int32)

    tables = row_tables(ids, width)
    if lax.axis_size("read") == 2 and lax.axis_size("pair") == 2 and tiles == 4 and freqs == 4:
        gathered = fused(info, low, block, high, taps, tables, freqs)
    else:
        terms = front(info, low, block, high, taps, tables)
        if tiles != readers:
            terms = terms.reshape(tiles, rows_dev, 2, 2, readers // tiles, TILE * tiles // readers)
            terms = terms.transpose(0, 4, 1, 2, 3, 5).reshape(readers, rows_dev, -1)
        summed = lax.psum_scatter(terms, READERS, scatter_dimension=0, tiled=True)
        summed = summed.reshape(rows_dev, 2, 2, freqs, share // 2)
        summed = summed.transpose(3, 0, 2, 1, 4).reshape(freqs, rows_dev, 2 * share)
        gathered = lax.all_to_all(summed, "freq", split_axis=0, concat_axis=0, tiled=True)
    grid = columns(gathered.reshape(height, 2 * share), order_matrix(share), column_tables(height))
    grid = lax.all_to_all(
        grid.reshape(readers, out_rows, 2 * share), READERS, split_axis=0, concat_axis=0, tiled=True
    )
    numer = grid.reshape(readers, out_rows, 2, share).transpose(2, 1, 0, 3)
    numer = numer.reshape(2, out_rows, per_freq)

    all_u = angles(np.arange(height), offsets, height)
    all_rows = np.concatenate([np.cos(all_u), np.sin(all_u)], axis=1).astype(np.float32)
    psf_rows = lax.dynamic_slice_in_dim(jnp.asarray(all_rows), reader_at * out_rows, out_rows, 0)
    all_v = angles(offsets, np.arange(width // 2), width)
    all_cols = np.stack([np.cos(all_v), -np.sin(all_v)]).astype(np.float32)
    own_cols = lax.dynamic_slice_in_dim(jnp.asarray(all_cols), freq_at * per_freq, per_freq, 2)
    q = jnp.einsum("nab,cbp->cnap", stamps, own_cols, precision=HIGHEST)
    psf_cols = jnp.concatenate(
        [jnp.concatenate([q[0], q[1]], axis=2), jnp.concatenate([q[1], -q[0]], axis=2)], axis=1
    )
    inverse = pl.pallas_call(
        denom_kernel,
        out_shape=jax.ShapeDtypeStruct((out_rows, per_freq), F32),
        in_specs=[
            pl.BlockSpec(memory_space=pltpu.SMEM),
            pl.BlockSpec(memory_space=pltpu.VMEM),
            pl.BlockSpec(memory_space=pltpu.VMEM),
        ],
        out_specs=pl.BlockSpec(memory_space=pltpu.VMEM),
        compiler_params=pltpu.CompilerParams(vmem_limit_bytes=32 * 1024 * 1024),
        name="denom",
    )(denom_weight, psf_rows, psf_cols)
    return numer * inverse


def solution(mesh):
    in_specs = (
        P(("groups", "read", "pair"), "freq", None),
        P("groups", None, None),
        P("groups"),
        P("groups"),
        P("groups", None),
        P("groups"),
        P("groups"),
    )
    out_specs = P(None, ("groups", "read", "pair"), "freq")
    return jax.shard_map(
        per_device, mesh=mesh, in_specs=in_specs, out_specs=out_specs, check_vma=False
    )
```

profile of v0, /device:TPU:1, one launch (start us, length us, event | category | flops | bytes accessed | tf_op | source)
XLA Modules:
  0.0 104.5 jit_solution(1182715575013850175)
XLA Ops:
  0.0 1.0 slice_bitcast_fusion
  1.0 2.2 %collective-permute-start = (f32[16,2048]{1,0:T(8,128)S(1)}, f32[16,2048]{1,0:T(8,128)S(1)}, u32[]{:S(2)}, u32[]{:S(2)}) collective-permute-start(f32[16,2048]{1,0:T(8,128)S(1)} %get-tuple-element.8), channel_id=1, source_target_pairs={{0,4},{4,8},{8,12},{12,0},{1,5},{5,9},{9,13},{13,1},{2,6},{6,10},{... | collective-permute-start | bytes 393224 | tf_op jit(solution)/shard_map/ppermute | solution.py:494
  3.2 2.1 %collective-permute-start.1 = (f32[16,2048]{1,0:T(8,128)S(1)}, f32[16,2048]{1,0:T(8,128)S(1)}, u32[]{:S(2)}, u32[]{:S(2)}) collective-permute-start(f32[16,2048]{1,0:T(8,128)S(1)} %get-tuple-element.7), channel_id=1, source_target_pairs={{4,0},{8,4},{12,8},{0,12},{5,1},{9,5},{13,9},{1,13},{6,2},{10,6},{... | collective-permute-start | bytes 393224 | tf_op jit(solution)/shard_map/ppermute | solution.py:495
  5.3 1.3 %fusion.6 = s32[]{:T(128)} fusion(s32[4]{0:T(128)} %param.21, s32[]{:T(128)S(6)} %add.9), kind=kLoop, calls=%fused_computation.17 | loop fusion | flops 11 | bytes 24 | tf_op jit(solution)/shard_map/reduce_sum | solution.py:498
  6.6 0.6 iota_compare_fusion
  7.2 2.1 %fusion.8 = (s32[]{:T(128)}, s32[]{:T(128)}) fusion(s32[4,2]{0,1:T(2,128)} %param.19, s32[]{:T(128)} %fusion.6), kind=kLoop, calls=%fused_computation.22 | loop fusion | flops 18 | bytes 44 | tf_op jit(solution)/shard_map/reduce_sum | solution.py:500
  9.3 0.8 select_reduce_fusion
  10.2 2.0 %multiply_divide_fusion = (f32[4]{0:T(128)S(1)}, f32[]{:T(128)}) fusion(f32[4]{0:T(128)} %param.18, f32[4]{0:T(128)} %param.17, s32[4]{0:T(128)} %param.20, s32[]{:T(128)} %fusion.6), kind=kLoop, calls=%fused_computation.23 | loop fusion | flops 31 | bytes 72 | tf_op jit(solution)/shard_map/div | solution.py:504
  12.8 1.2 %convolution_bitcast_fusion = f32[2,16,1024]{2,1,0:T(8,128)S(1)} fusion(f32[2,16,1024]{2,1,0:T(8,128)} %constant.45.clone, f32[16,16]{1,0:T(8,128)S(1)} %select_reduce_fusion, f32[]{:T(128)S(6)} %mul.39), kind=kOutput, calls=%fused_computation | convolution fusion | flops 6291712 | bytes 263172 | tf_op jit(solution)/shard_map/ab,cbp->cap/dot_general | solution.py:510
  14.0 1.9 %pad_add_fusion.info = s32[4]{0:T(128)} fusion(s32[1]{0:T(128)} %constant.19.clone.1, s32[1]{0:T(128)} %bitcast.4, s32[1]{0:T(128)} %bitcast.2, s32[1]{0:T(128)} %bitcast), kind=kLoop, calls=%fused_computation.18 | loop fusion | flops 12 | bytes 32 | tf_op jit(solution)/shard_map/stack | solution.py:512
  15.8 0.1 reshape.22
  15.9 0.7 copy.24
  16.6 1.0 constant_dynamic-slice_fusion.rows
  17.6 0.0 collective-permute-done.low
  17.6 0.0 copy-start.3
  17.6 0.0 collective-permute-done.1.high
  17.6 0.0 copy-start.4
  17.6 0.6 copy-done.3
  18.2 0.0 copy-done.4
  18.3 54.2 %fused.1 = f32[4,512,128]{2,1,0:T(8,128)} custom-call(s32[4]{0:T(128)} %pad_add_fusion.info, f32[16,2048]{1,0:T(8,128)} %copy-done.3, f32[512,2048]{1,0:T(8,128)} %bitcast.52, f32[16,2048]{1,0:T(8,128)} %copy-done.4, f32[4,2,2,16,128]{4,3,2,1,0:T(8,128)} %bitcast.51, bf16[4,2,1024,256]{3,2,1,0:T(8,128)(2,1)} %constant.46.clone.th, ...), custom_call_target="tpu_custom_call" | custom-call | flops 7000000000 | bytes 14680064 | tf_op jit(solution)/shard_map/fused/pallas_call | solution.py:359
  72.5 1.2 %copy-done = f32[4,512,128]{2,1,0:T(8,128)S(1)} copy-done((f32[4,512,128]{2,1,0:T(8,128)S(1)}, f32[4,512,128]{2,1,0:T(8,128)}, u32[]{:S(2)}) %copy-start) | copy-done | bytes 1048600
  73.7 8.2 %columns.1 = f32[2048,128]{1,0:T(8,128)S(1)} custom-call(f32[2048,128]{1,0:T(8,128)S(1)} %bitcast.49, bf16[128,256]{1,0:T(8,128)(2,1)S(1)} %copy-done.1, bf16[4,512,1024]{2,1,0:T(8,128)(2,1)} %constant.49.clone.th, bf16[4,512,1024]{2,1,0:T(8,128)(2,1)} %constant.50.clone.tl), custom_call_target="tpu_custom_call" | custom-call | tf_op jit(solution)/shard_map/columns/pallas_call | solution.py:447
  81.9 0.0 copy-start.2
  81.9 1.3 %copy.18 = f32[4,512,128]{1,2,0:T(8,128)} copy(f32[4,512,128]{2,1,0:T(8,128)S(1)} %bitcast.48) | data formatting | bytes 2097152 | tf_op jit(solution)/shard_map/reshape | solution.py:528
  83.3 6.0 %all-to-all-start = ((f32[4,512,128]{1,2,0:T(8,128)}), f32[4,512,128]{1,2,0:T(8,128)S(1)}, u32[]{:S(2)}, u32[]{:S(2)}) async-start(f32[4,512,128]{1,2,0:T(8,128)} %copy.18), calls=%async_computation | async-start | bytes 2097152 | tf_op jit(solution)/shard_map/all_to_all | solution.py:527
  89.3 1.0 convolution_bitcast_fusion.1
  90.4 2.3 %denom.1 = f32[512,256]{1,0:T(8,128)S(1)} custom-call(f32[4]{0:T(128)S(1)} %get-tuple-element.11.weight, f32[512,32]{1,0:T(8,128)S(1)} %constant_dynamic-slice_fusion.rows, f32[4,32,512]{2,1,0:T(8,128)S(1)} %maximum_maximum_fusion.cols), custom_call_target="tpu_custom_call" | custom-call | tf_op jit(solution)/shard_map/denom/pallas_call | solution.py:543
  92.7 0.2 copy.20
  92.9 10.0 %all-to-all-done = f32[4,512,128]{1,2,0:T(8,128)S(1)} async-done(((f32[4,512,128]{1,2,0:T(8,128)}), f32[4,512,128]{1,2,0:T(8,128)S(1)}, u32[]{:S(2)}, u32[]{:S(2)}) %all-to-all-start) | async-done | bytes 1048608 | tf_op jit(solution)/shard_map/all_to_all | solution.py:527
  102.9 0.1 copy.19
  103.0 0.2 bitcast_multiply_fusion
  103.2 1.3 %copy.21 = f32[2,512,256]{2,1,0:T(8,128)} copy(f32[2,512,256]{1,2,0:T(8,128)S(1)} %bitcast_multiply_fusion) | data formatting | bytes 2097152 | tf_op jit(solution)/shard_map/mul | solution.py:555
  (7 shorter events, 0.0 us)
Async XLA Ops:
  1.0 16.6 %collective-permute-start = (f32[16,2048]{1,0:T(8,128)S(1)}, f32[16,2048]{1,0:T(8,128)S(1)}, u32[]{:S(2)}, u32[]{:S(2)}) collective-permute-start(f32[16,2048]{1,0:T(8,128)S(1)} %get-tuple-element.8), channel_id=1, source_target_pairs={{0,4},{4,8},{8,12},{12,0},{1,5},{5,9},{9,13},{13,1},{2,6},{6,10},{... | collective-permute-start | bytes 393224 | tf_op jit(solution)/shard_map/ppermute | solution.py:494
  3.2 14.4 %collective-permute-start.1 = (f32[16,2048]{1,0:T(8,128)S(1)}, f32[16,2048]{1,0:T(8,128)S(1)}, u32[]{:S(2)}, u32[]{:S(2)}) collective-permute-start(f32[16,2048]{1,0:T(8,128)S(1)} %get-tuple-element.7), channel_id=1, source_target_pairs={{4,0},{8,4},{12,8},{0,12},{5,1},{9,5},{13,9},{1,13},{6,2},{10,6},{... | collective-permute-start | bytes 393224 | tf_op jit(solution)/shard_map/ppermute | solution.py:495
  17.6 0.7 copy-start.3
  17.6 0.7 copy-start.4
  18.3 54.3 %copy-start.1 = (bf16[128,256]{1,0:T(8,128)(2,1)S(1)}, bf16[128,256]{1,0:T(8,128)(2,1)}, u32[]{:S(2)}) copy-start(bf16[128,256]{1,0:T(8,128)(2,1)} %constant.48.clone.order) | copy-start | bytes 196612
  72.5 1.2 %copy-start = (f32[4,512,128]{2,1,0:T(8,128)S(1)}, f32[4,512,128]{2,1,0:T(8,128)}, u32[]{:S(2)}) copy-start(f32[4,512,128]{2,1,0:T(8,128)} %fused.1) | copy-start | bytes 3145732
  81.9 7.4 %copy-start.2 = (f32[4,16,16]{2,1,0:T(8,128)S(1)}, f32[4,16,16]{2,1,0:T(8,128)}, u32[]{:S(2)}) copy-start(f32[4,16,16]{2,1,0:T(8,128)} %param.16) | copy-start | bytes 12292
  83.3 19.6 %all-to-all-start = ((f32[4,512,128]{1,2,0:T(8,128)}), f32[4,512,128]{1,2,0:T(8,128)S(1)}, u32[]{:S(2)}, u32[]{:S(2)}) async-start(f32[4,512,128]{1,2,0:T(8,128)} %copy.18), calls=%async_computation | async-start | bytes 2097152 | tf_op jit(solution)/shard_map/all_to_all | solution.py:527
where the time goes:
time: 106 us; the launch traced here: 104 us
  Pallas kernels  64.7 us (61%)
  starting transfers between devices  10.3 us (10%)
  waiting for transfers between devices  10 us (9%)
  other arithmetic  8.97 us (8%)
  local copies, waits for them, and re-layouts  7.49 us (7%)
  matrix products  2.16 us (2%)
    pallas_call x1, Pallas kernels, fused(): pl.pallas_call(functools.partial(fused_kernel, freqs), out_shape=jax.Shap...  54.2 us
    all_to_all x1, waiting for transfers between devices, per_device(): lax.all_to_all(grid.reshape(readers, out_rows, 2 * share), READERS, split...  10 us
    pallas_call x1, Pallas kernels, columns(): pl.pallas_call(column_kernel, grid=(4,), out_shape=jax.ShapeDtypeStruct((...  8.18 us
    all_to_all x1, starting transfers between devices, per_device(): lax.all_to_all(grid.reshape(readers, out_rows, 2 * share), READERS, split...  6.04 us
    pallas_call x1, Pallas kernels, per_device(): pl.pallas_call(denom_kernel, out_shape=jax.ShapeDtypeStruct((out_rows, pe...  2.32 us
    ppermute x1, starting transfers between devices, per_device(): low = lax.ppermute(block[rows_dev - HALO:], 'freq', forward)  2.18 us
  transfers between devices with their start and end apart: 3, of which 1 were waited for; matrix products, arithmetic and copies ran while one was open for 12% of the time, Pallas kernels for 2%

commit v1 on v0

--- a/solution.py
+++ b/solution.py
@@ -159,234 +159,536 @@
     )(info, low, block, high, taps, *tables)
 
 
+MESH = pl.DeviceIdType.MESH
 CHUNKS = 4
-MESH = pl.DeviceIdType.MESH
-
-
-def clean_rows(info, low, block, high, ext, ch, cl, height):
+LANES = 128
+
+
+def joint_columns(width):
+    per_freq = width // 2 // 4
+    freq = np.arange(4)[:, None] * per_freq
+    inner = np.arange(32)[None, :]
+    groups = []
+    for k in range(2):
+        for rd in range(2):
+            for pd in range(2):
+                if k == 0:
+                    ids = freq + 4 * (32 * rd + inner) + 2 * pd
+                else:
+                    ids = freq + 64 * (2 * rd + pd) + 2 * inner + 1
+                groups.append(ids.reshape(-1))
+    return np.stack(groups)
+
+
+def joint_row_tables(ids, width):
+    even, odd = [], []
+    for t in range(8):
+        depth = width // 4 if t < 4 else width // 2
+        phase = angles(np.arange(depth), ids[t], width)
+        table = np.concatenate([np.cos(phase), -np.sin(phase)], axis=1)
+        (even if t < 4 else odd).append(table)
+    return split_np(np.stack(even)) + split_np(np.stack(odd))
+
+
+def joint_column_tables(height):
+    inner = np.arange(256)
+    parts = []
+    for g in range(8):
+        phase = angles(np.arange(256), 8 * inner + g, height)
+        parts.append(np.concatenate([np.cos(phase), np.sin(phase)], axis=1))
+    return split_np(np.stack(parts))
+
+
+def joint_twiddles():
+    lane = np.arange(LANES)
+    table = np.zeros((4, 8, LANES), np.float32)
+    for gg in range(4):
+        angle = np.where(lane >= 64, TWO_PI * gg / 8, 0.0)
+        real = lane % 64 < 32
+        table[gg, 0] = np.cos(angle)
+        table[gg, 1] = np.where(real, np.sin(angle), 0.0)
+        table[gg, 2] = np.where(real, 0.0, -np.sin(angle))
+        table[gg, 3] = np.where(lane < 64, 1.0, -1.0)
+    return table
+
+
+def joint_order(ids, width):
+    per_freq = width // 2 // 4
+    table = np.zeros((256, 256), np.float32)
+    for k in range(2):
+        for reader in range(4):
+            for i in range(32):
+                table[k * LANES + reader * 32 + i, ids[4 * k + reader, i] % per_freq] = 1.0
+    return table.astype(ml_dtypes.bfloat16)
+
+
+def joint_psf_tables(height, width, stamp_len):
+    offsets = np.arange(stamp_len) - stamp_len // 2
+    all_u = angles(np.arange(height), offsets, height)
+    hi, lo = split_np(np.concatenate([np.cos(all_u), np.sin(all_u)], axis=1))
+    rows = np.concatenate([hi, lo, hi, np.zeros_like(hi)], axis=1).reshape(4, height // 4, LANES)
+    all_v = angles(offsets, np.arange(width // 2), width).reshape(stamp_len, 4, -1)
+    cols = np.concatenate([np.cos(all_v), -np.sin(all_v)], axis=2).astype(np.float32)
+    return rows, cols.transpose(1, 0, 2)
+
+
+def joint_tap_table(ids, width, stamp_len):
+    offsets = np.arange(stamp_len) - stamp_len // 2
+    phase = [angles(offsets, ids[t], width) for t in range(8)]
+    return np.stack(
+        [np.concatenate([np.cos(x), -np.sin(x)], axis=1) for x in phase]
+    ).astype(np.float32)
+
+
+def turn(quads, lanes):
+    low = lanes < 64
+    first = [None] * 4
+    for q in range(2):
+        first[q] = jnp.where(low, quads[q], pltpu.roll(quads[q + 2], 64, 1))
+        first[q + 2] = jnp.where(low, pltpu.roll(quads[q], 64, 1), quads[q + 2])
+    even = lanes % 64 < 32
+    result = [None] * 4
+    for q in (0, 2):
+        result[q] = jnp.where(even, first[q], pltpu.roll(first[q + 1], 32, 1))
+        result[q + 1] = jnp.where(even, pltpu.roll(first[q], 96, 1), first[q + 1])
+    return result
+
+
+def joint_kernel(
+    zero_point, noise_var, footprint, accept, assign, stamps, block, tap_table,
+    th0, tl0, th1, tl1, cth, ctl, twiddle, order, psf_rows, psf_cols, out,
+    ext, ch0, cl0, ch1, cl1, grid, taps,
+    bh0, bl0, bh1, bl1, ch_tab, cl_tab, prow, inverse,
+    work, pair_in, read_in, freq_out, freq_in, mixed, col_out, col_in,
+    block_sem, table_sem, halo_send, halo_recv, pair_send, pair_recv,
+    read_send, read_recv, freq_send, freq_recv, col_send, col_recv,
+):
     rows, width = block.shape
+    freqs = 4
+    height = rows * freqs
+    quarter = width // 4
     half = width // 2
-    ext[:HALO] = low[...]
-    ext[HALO : HALO + rows] = block[...]
-    ext[HALO + rows :] = high[...]
+    r = lax.axis_index("read")
+    p = lax.axis_index("pair")
+    f = lax.axis_index("freq")
+    me = 2 * r + p
+
+    def group_at(s):
+        rd = jnp.where(s < 2, 1 - r, r)
+        pd = jnp.where(s % 2 == 0, 1 - p, p)
+        return rd * 2 + pd
+
+    def block_copy(n):
+        size = rows // 4
+        return pltpu.make_async_copy(
+            block.at[pl.ds(n * size, size)], ext.at[pl.ds(HALO + n * size, size)], block_sem.at[n]
+        )
+
+    def row_table_copies(k, s):
+        t = group_at(s)
+        pairs = ((th0, bh0), (tl0, bl0)) if k == 0 else ((th1, bh1), (tl1, bl1))
+        return [
+            pltpu.make_async_copy(a.at[t], b.at[s], table_sem.at[k, n, s])
+            for n, (a, b) in enumerate(pairs)
+        ]
+
+    def column_table_copies():
+        return (
+            pltpu.make_async_copy(cth, ch_tab, table_sem.at[2, 0, 0]),
+            pltpu.make_async_copy(ctl, cl_tab, table_sem.at[2, 0, 1]),
+        )
+
+    def psf_copy():
+        return pltpu.make_async_copy(psf_rows.at[me], prow, table_sem.at[2, 0, 2])
+
+    def halo_copies():
+        up = lax.rem(f + 1, freqs)
+        down = lax.rem(f + freqs - 1, freqs)
+        return (
+            pltpu.make_async_remote_copy(
+                src_ref=block.at[pl.ds(rows - HALO, HALO)], dst_ref=ext.at[pl.ds(0, HALO)],
+                send_sem=halo_send.at[0], recv_sem=halo_recv.at[0],
+                device_id={"freq": up}, device_id_type=MESH,
+            ),
+            pltpu.make_async_remote_copy(
+                src_ref=block.at[pl.ds(0, HALO)], dst_ref=ext.at[pl.ds(HALO + rows, HALO)],
+                send_sem=halo_send.at[1], recv_sem=halo_recv.at[1],
+                device_id={"freq": down}, device_id_type=MESH,
+            ),
+        )
+
+    chunk = rows // CHUNKS
+
+    def pair_copy(k, n, c):
+        part = pl.ds(pl.multiple_of(c * chunk, chunk), chunk)
+        return pltpu.make_async_remote_copy(
+            src_ref=work.at[k, 2 * n, part], dst_ref=pair_in.at[k, n, part],
+            send_sem=pair_send.at[k, n, c], recv_sem=pair_recv.at[k, n, c],
+            device_id={"pair": 1 - p}, device_id_type=MESH,
+        )
+
+    def read_copy(k, c):
+        part = pl.ds(pl.multiple_of(c * chunk, chunk), chunk)
+        return pltpu.make_async_remote_copy(
+            src_ref=work.at[k, 1, part], dst_ref=read_in.at[k, part],
+            send_sem=read_send.at[k, c], recv_sem=read_recv.at[k, c],
+            device_id={"read": 1 - r}, device_id_type=MESH,
+        )
+
+    def freq_copy(k, d, c):
+        part = pl.ds(2 * c, 2)
+        to = lax.rem(f + d, freqs)
+        return pltpu.make_async_remote_copy(
+            src_ref=freq_out.at[k, to, part], dst_ref=freq_in.at[k, f, part],
+            send_sem=freq_send.at[k, d - 1, c], recv_sem=freq_recv.at[k, d - 1, c],
+            device_id={"freq": to}, device_id_type=MESH,
+        )
+
+    def col_copy(k, n):
+        rd = 1 - r if n > 0 else r
+        pd = p if n == 1 else 1 - p
+        return pltpu.make_async_remote_copy(
+            src_ref=col_out.at[k, 2 * rd + pd], dst_ref=col_in.at[k, me],
+            send_sem=col_send.at[k, n], recv_sem=col_recv.at[k, n],
+            device_id={"read": rd, "pair": pd}, device_id_type=MESH,
+        )
+
+    barrier = pltpu.get_barrier_semaphore()
+    for d in range(1, freqs):
+        pl.semaphore_signal(
+            barrier, inc=1, device_id={"freq": lax.rem(f + d, freqs)}, device_id_type=MESH
+        )
+    for rd, pd in ((r, 1 - p), (1 - r, p), (1 - r, 1 - p)):
+        pl.semaphore_signal(
+            barrier, inc=1, device_id={"read": rd, "pair": pd}, device_id_type=MESH
+        )
+    for n in range(4):
+        block_copy(n).start()
+    for k in range(2):
+        for s in range(4):
+            for copy in row_table_copies(k, s):
+                copy.start()
+    for copy in column_table_copies():
+        copy.start()
+    psf_copy().start()
+
+    mine = assign[me]
+    first_row = footprint[0, mine]
+    last_row = footprint[1, mine]
+    scale = 1.0 / math.sqrt(height * width)
+    top = accept[mine].astype(F32) * zero_point[mine] * scale
+    side = stamps.shape[1]
+    stamp = stamps[mine] * (jnp.full((side, side), top, F32) / jnp.full((side, side), noise_var[mine], F32))
+    for t in range(8):
+        both = jnp.dot(stamp, tap_table[t], precision=HIGHEST, preferred_element_type=F32)
+        taps[t, 0] = both[:, :LANES]
+        taps[t, 1] = both[:, LANES:]
+
+    pl.semaphore_wait(barrier, freqs + 2)
+    for copy in halo_copies():
+        copy.start()
+
     cols = lax.broadcasted_iota(jnp.int32, (16, width), 1)
 
     def clean(i, carry):
         at = pl.multiple_of(i * 16, 16)
         piece = ext[pl.ds(at, 32), :]
         mid = piece[8:24]
-        ids = info[0] - 8 + at + lax.broadcasted_iota(jnp.int32, (16, 1), 0)
+        ids = f * rows - 8 + at + lax.broadcasted_iota(jnp.int32, (16, 1), 0)
         ids = jnp.where(ids < 0, ids + height, ids)
         ids = jnp.where(ids >= height, ids - height, ids)
         up = jnp.where(ids == 0, 0.0, piece[7:23])
         down = jnp.where(ids == height - 1, 0.0, piece[9:25])
         left = jnp.where(cols == 0, 0.0, pltpu.roll(mid, 1, 1))
         right = jnp.where(cols == width - 1, 0.0, pltpu.roll(mid, width - 1, 1))
-        inside = (ids >= info[1]) & (ids < info[2])
+        inside = (ids >= first_row) & (ids < last_row)
         cell = jnp.where(inside, mid - 0.25 * (up + down + left + right), 0.0)
-        for parity in range(2):
-            if parity == 0:
-                fold = cell[:, :half] + cell[:, half:]
+        total = cell[:, :half] + cell[:, half:]
+        here = pl.ds(at, 16)
+        hi, lo = split(cell[:, :half] - cell[:, half:])
+        ch1[here, :] = hi
+        cl1[here, :] = lo
+        hi, lo = split(total[:, :quarter] + total[:, quarter:])
+        ch0[0, here, :] = hi
+        cl0[0, here, :] = lo
+        hi, lo = split(total[:, :quarter] - total[:, quarter:])
+        ch0[1, here, :] = hi
+        cl0[1, here, :] = lo
+        return carry
+
+    for n in range(4):
+        block_copy(n).wait()
+    lax.fori_loop(1, rows // 16, clean, 0)
+    for copy in halo_copies():
+        copy.wait_recv()
+    clean(0, 0)
+    clean(rows // 16, 0)
+
+    lanes = lax.broadcasted_iota(jnp.int32, (32, LANES), 1)
+
+    def pack(k, c):
+        read_copy(k, c).wait_recv()
+        pair_copy(k, 1, c).wait_recv()
+
+        def body(n, carry):
+            b = 2 * c + n
+            quads = []
+            for g in range(2):
+                here = pl.ds(pl.multiple_of(b * 64 + g * 32, 32), 32)
+                total = work[k, 3, here, :] + pair_in[k, 1, here, :] + read_in[k, here, :]
+                quads += [total[:, :LANES], total[:, LANES:]]
+            for to, value in enumerate(turn(quads, lanes)):
+                freq_out[k, to, b] = value.reshape(4, 8, LANES)
+            return carry
+
+        lax.fori_loop(0, 2, body, 0)
+        for d in range(1, freqs):
+            freq_copy(k, d, c).start()
+
+    def groups(k):
+        def step(s, carry):
+            for copy in row_table_copies(k, s):
+                copy.wait()
+            t = group_at(s)
+            if k == 0:
+                xh, xl, wh, wl = ch0[t % 2], cl0[t % 2], bh0[s], bl0[s]
             else:
-                fold = cell[:, :half] - cell[:, half:]
-            hi, lo = split(fold)
-            ch[parity, pl.ds(at, 16), :] = hi
-            cl[parity, pl.ds(at, 16), :] = lo
+                xh, xl, wh, wl = ch1[...], cl1[...], bh1[s], bl1[s]
+            both = dot(xh, wh) + dot(xh, wl) + dot(xl, wh)
+            grid[0] = both[:, :LANES]
+            grid[1] = both[:, LANES:]
+
+            def fir(c, inner):
+                for n in range(2):
+                    at = pl.multiple_of(c * chunk + n * 64, 64)
+                    sums = [[jnp.zeros((8, LANES), F32), jnp.zeros((8, LANES), F32)] for _ in range(8)]
+                    for a in range(16):
+                        qr = taps[4 * k + t, 0, a : a + 1, :]
+                        qi = taps[4 * k + t, 1, a : a + 1, :]
+                        for g in range(8):
+                            here = pl.ds(at + g + a, 8, stride=8)
+                            xr = grid[0, here, :]
+                            xi = grid[1, here, :]
+                            sums[g][0] = sums[g][0] + (qr * xr + qi * xi)
+                            sums[g][1] = sums[g][1] + (qr * xi - qi * xr)
+                    for g in range(8):
+                        work[k, s, pl.ds(at + 8 * g, 8), :LANES] = sums[g][0]
+                        work[k, s, pl.ds(at + 8 * g, 8), LANES:] = sums[g][1]
+
+                @pl.when(s == 0)
+                def _():
+                    pair_copy(k, 0, c).start()
+
+                @pl.when(s == 2)
+                def _():
+                    pair_copy(k, 1, c).start()
+
+                @pl.when(s == 1)
+                def _():
+                    pair_copy(k, 0, c).wait_recv()
+                    part = pl.ds(pl.multiple_of(c * chunk, chunk), chunk)
+                    work[k, 1, part, :] = work[k, 1, part, :] + pair_in[k, 0, part, :]
+                    read_copy(k, c).start()
+
+                return inner
+
+            lax.fori_loop(0, CHUNKS, fir, 0)
+            if k == 1:
+
+                @pl.when(s < 3)
+                def _():
+                    pack(0, s + 1)
+
+            return carry
+
+        lax.fori_loop(0, 4, step, 0)
+
+    def times_j(x, at):
+        real = at % 64 < 32
+        return jnp.where(real, pltpu.roll(x, 96, 1), -pltpu.roll(x, 32, 1))
+
+    def columns(k):
+        for d in range(1, freqs):
+            for c in range(CHUNKS):
+                freq_copy(k, d, c).wait_recv()
+        freq_in[k, f] = freq_out[k, f]
+        wide = lax.broadcasted_iota(jnp.int32, (256, LANES), 1)
+
+        def body(gg, carry):
+            x = freq_in[k, :, :, gg].reshape(256, LANES)
+            hi, lo = split(jnp.concatenate([x, times_j(x, wide)], axis=0))
+            rhs = jnp.concatenate([hi, lo], axis=1)
+            sides = []
+            for g in (gg, gg + 4):
+                res = dot(ch_tab[g], rhs)
+                sides.append(res[:, :LANES] + res[:, LANES:] + dot(cl_tab[g], hi))
+            both = jnp.where(wide < 64, sides[0], sides[1])
+            both = pltpu.roll(both, 64, 1) + both * twiddle[gg, 3:4, :]
+            mixed[gg] = (
+                both * twiddle[gg, 0:1, :]
+                + pltpu.roll(both, 96, 1) * twiddle[gg, 1:2, :]
+                + pltpu.roll(both, 32, 1) * twiddle[gg, 2:3, :]
+            )
+            return carry
+
+        lax.fori_loop(0, 4, body, 0)
+
+        def last(i, carry):
+            here = pl.ds(pl.multiple_of(i * 32, 32), 32)
+            e = [mixed[gg, here, :] for gg in range(4)]
+            a, b = e[0] + e[2], e[1] + e[3]
+            c, d = e[0] - e[2], times_j(e[1] - e[3], lanes)
+            col_out[k, 0, here, :] = a + b
+            col_out[k, 1, here, :] = c + d
+            col_out[k, 2, here, :] = a - b
+            col_out[k, 3, here, :] = c - d
+            return carry
+
+        lax.fori_loop(0, 8, last, 0)
+
+    def denominator():
+        psf_copy().wait()
+        count = stamps.shape[0]
+        sides = []
+        weights = []
+        for e in range(count):
+            q = jnp.dot(stamps[e], psf_cols[f], precision=HIGHEST, preferred_element_type=F32)
+            turned = jnp.concatenate([q[:, 256:], -q[:, :256]], axis=1)
+            hi, lo = split(jnp.concatenate([q, turned], axis=0))
+            sides.append(jnp.concatenate([hi, hi, lo, jnp.zeros_like(hi)], axis=0))
+            value = accept[e].astype(F32) * zero_point[e] * zero_point[e]
+            weights.append(jnp.full((1, 256), value, F32) / jnp.full((1, 256), noise_var[e], F32))
+        for n in range(4):
+            here = pl.ds(n * 128, 128)
+            total = jnp.zeros((128, 256), F32)
+            for e in range(count):
+                psf = dot(prow[here, :], sides[e])
+                re, im = psf[:, :256], psf[:, 256:]
+                total = total + weights[e] * (re * re + im * im)
+            inverse[here, :] = lax.rsqrt(total)
+
+    groups(0)
+    pack(0, 0)
+    groups(1)
+    denominator()
+    for copy in column_table_copies():
+        copy.wait()
+    columns(0)
+    col_copy(0, 0).start()
+
+    def rest(c, carry):
+        pack(1, c)
         return carry
 
-    lax.fori_loop(0, (rows + 16) // 16, clean, 0)
-
-
-def fused_kernel(
-    freqs, info, low, block, high, taps, th, tl, out,
-    ext, ch, cl, grid, bufh, bufl, work, pair_in, read_in, freq_out, freq_in,
-    table_sem, pair_send, pair_recv, read_send, read_recv, freq_send, freq_recv,
-):
+    lax.fori_loop(0, CHUNKS, rest, 0)
+    col_copy(0, 1).start()
+    col_copy(0, 2).start()
+    columns(1)
+    for n in range(3):
+        col_copy(1, n).start()
+    for k in range(2):
+        col_in[k, me] = col_out[k, me]
+        for n in range(3):
+            col_copy(k, n).wait_recv()
+
+    wide = lax.broadcasted_iota(jnp.int32, (64, LANES), 1)
+
+    def finish(i, carry):
+        at = pl.multiple_of(i * 64, 64)
+        parts = []
+        for k in range(2):
+            quads = [col_in[k, n, pl.ds(at, 64), :] for n in range(4)]
+            parts.append(jnp.concatenate(turn(quads, wide), axis=0))
+        hi, lo = split(jnp.concatenate(parts, axis=1))
+        result = dot(hi, order[...]) + dot(lo, order[...])
+        for q in range(4):
+            here = pl.ds(256 * (q // 2) + at, 64)
+            out[q % 2, here, :] = result[64 * q : 64 * (q + 1)] * inverse[here, :]
+        return carry
+
+    lax.fori_loop(0, 4, finish, 0)
+
+    for copy in halo_copies():
+        copy.wait_send()
+    for k in range(2):
+        for c in range(CHUNKS):
+            for n in range(2):
+                pair_copy(k, n, c).wait_send()
+            read_copy(k, c).wait_send()
+            for d in range(1, freqs):
+                freq_copy(k, d, c).wait_send()
+        for n in range(3):
+            col_copy(k, n).wait_send()
+
+
+def joint(block, stamps, zero_point, noise_var, footprint, accept, assign):
     rows, width = block.shape
-    height = rows * freqs
-    chunk = rows // CHUNKS
-    share = TILE // freqs
-    r = lax.axis_index("read")
-    p = lax.axis_index("pair")
-    f = lax.axis_index("freq")
-
-    def tile_at(s):
-        rd = jnp.where(s < 2, 1 - r, r)
-        pd = jnp.where(s % 2 == 0, 1 - p, p)
-        return rd * 2 + pd
-
-    def table_copies(s):
-        t = tile_at(s)
-        return (
-            pltpu.make_async_copy(th.at[t], bufh.at[s], table_sem.at[0, s]),
-            pltpu.make_async_copy(tl.at[t], bufl.at[s], table_sem.at[1, s]),
-        )
-
-    def pair_copy(n):
-        return pltpu.make_async_remote_copy(
-            src_ref=work.at[2 * n], dst_ref=pair_in.at[n],
-            send_sem=pair_send.at[n], recv_sem=pair_recv.at[n],
-            device_id={"pair": 1 - p}, device_id_type=MESH,
-        )
-
-    def read_copy(c):
-        part = pl.ds(c * chunk, chunk)
-        return pltpu.make_async_remote_copy(
-            src_ref=work.at[1, part], dst_ref=read_in.at[part],
-            send_sem=read_send.at[c], recv_sem=read_recv.at[c],
-            device_id={"read": 1 - r}, device_id_type=MESH,
-        )
-
-    def freq_copy(d, c):
-        part = pl.ds(c * chunk, chunk)
-        to = lax.rem(f + d, freqs)
-        return pltpu.make_async_remote_copy(
-            src_ref=freq_out.at[to, part], dst_ref=freq_in.at[f, part],
-            send_sem=freq_send.at[d - 1, c], recv_sem=freq_recv.at[d - 1, c],
-            device_id={"freq": to}, device_id_type=MESH,
-        )
-
-    for s in range(4):
-        for copy in table_copies(s):
-            copy.start()
-    barrier = pltpu.get_barrier_semaphore()
-    pl.semaphore_signal(barrier, inc=1, device_id={"pair": 1 - p}, device_id_type=MESH)
-    pl.semaphore_signal(barrier, inc=1, device_id={"read": 1 - r}, device_id_type=MESH)
-    for d in range(1, freqs):
-        pl.semaphore_signal(
-            barrier, inc=1, device_id={"freq": lax.rem(f + d, freqs)}, device_id_type=MESH
-        )
-    clean_rows(info, low, block, high, ext, ch, cl, height)
-    pl.semaphore_wait(barrier, freqs + 1)
-
-    def step(s, carry):
-        for copy in table_copies(s):
-            copy.wait()
-        t = tile_at(s)
-        for parity in range(2):
-            grid[parity] = (
-                dot(ch[parity], bufh[s, parity])
-                + dot(ch[parity], bufl[s, parity])
-                + dot(cl[parity], bufh[s, parity])
-            )
-
-        def fir(i, inner):
-            at = pl.multiple_of(i * 32, 32)
-            for parity in range(2):
-                re = grid[parity, pl.ds(at, 48), :TILE]
-                im = grid[parity, pl.ds(at, 48), TILE:]
-                sum_re = jnp.zeros((32, TILE), F32)
-                sum_im = jnp.zeros((32, TILE), F32)
-                for k in range(8):
-                    shift_re = re[k : k + 40]
-                    shift_im = im[k : k + 40]
-                    for a in (k, k + 8):
-                        qr = taps[t, parity, 0, a : a + 1, :]
-                        qi = taps[t, parity, 1, a : a + 1, :]
-                        xr = shift_re[a - k : a - k + 32]
-                        xi = shift_im[a - k : a - k + 32]
-                        sum_re = sum_re + (qr * xr + qi * xi)
-                        sum_im = sum_im + (qr * xi - qi * xr)
-                lane = parity * 2 * TILE
-                work[s, pl.ds(at, 32), lane : lane + TILE] = sum_re
-                work[s, pl.ds(at, 32), lane + TILE : lane + 2 * TILE] = sum_im
-            return inner
-
-        lax.fori_loop(0, rows // 32, fir, 0)
-
-        @pl.when(s == 0)
-        def _():
-            pair_copy(0).start()
-
-        @pl.when(s == 1)
-        def _():
-            pair_copy(0).wait_recv()
-            for c in range(CHUNKS):
-                part = pl.ds(c * chunk, chunk)
-                work[1, part, :] = work[1, part, :] + pair_in[0, part, :]
-                read_copy(c).start()
-
-        @pl.when(s == 2)
-        def _():
-            pair_copy(1).start()
-
-        return carry
-
-    lax.fori_loop(0, 4, step, 0)
-
-    pair_copy(1).wait_recv()
-    lanes = lax.broadcasted_iota(jnp.int32, (32, TILE), 1) // share
-    for c in range(CHUNKS):
-        read_copy(c).wait_recv()
-
-        def pack(i, carry, c=c):
-            part = pl.ds(pl.multiple_of(c * chunk + i * 32, 32), 32)
-            total = work[3, part, :] + pair_in[1, part, :] + read_in[part, :]
-            quads = [
-                total[:, q * TILE : (q + 1) * TILE]
-                for q in (0, 2, 1, 3)
-            ]
-            for to in range(freqs):
-                result = None
-                for q in range(4):
-                    shift = (q - to) * share % TILE
-                    moved = quads[q] if shift == 0 else pltpu.roll(quads[q], shift, 1)
-                    result = moved if q == 0 else jnp.where(lanes == q, moved, result)
-                freq_out[to, part, :] = result
-            return carry
-
-        lax.fori_loop(0, chunk // 32, pack, 0)
-        for d in range(1, freqs):
-            freq_copy(d, c).start()
-    out[f] = freq_out[f]
-    for n in range(2):
-        pair_copy(n).wait_send()
-    for c in range(CHUNKS):
-        read_copy(c).wait_send()
-    for d in range(1, freqs):
-        for c in range(CHUNKS):
-            freq_copy(d, c).wait()
-        source = lax.rem(f + freqs - d, freqs)
-        out[source] = freq_in[source]
-
-
-def fused(info, low, block, high, taps, tables, freqs):
-    rows, width = block.shape
-    half = width // 2
+    height = 4 * rows
+    stamp_len = stamps.shape[1]
+    ids = joint_columns(width)
+    th0, tl0, th1, tl1 = joint_row_tables(ids, width)
+    cth, ctl = joint_column_tables(height)
+    psf_rows, psf_cols = joint_psf_tables(height, width, stamp_len)
     vmem = pl.BlockSpec(memory_space=pltpu.VMEM)
+    smem = pl.BlockSpec(memory_space=pltpu.SMEM)
     anywhere = pl.BlockSpec(memory_space=pl.ANY)
     dma = pltpu.SemaphoreType.DMA
+    half, quarter = width // 2, width // 4
     return pl.pallas_call(
-        functools.partial(fused_kernel, freqs),
-        out_shape=jax.ShapeDtypeStruct((freqs, rows, TILE), F32),
-        in_specs=[pl.BlockSpec(memory_space=pltpu.SMEM), vmem, vmem, vmem, vmem, anywhere, anywhere],
+        joint_kernel,
+        out_shape=jax.ShapeDtypeStruct((2, rows, 256), F32),
+        in_specs=[smem] * 5
+        + [vmem, anywhere, vmem]
+        + [anywhere] * 6
+        + [vmem, vmem, anywhere, vmem],
         out_specs=vmem,
         scratch_shapes=[
             pltpu.VMEM((rows + 2 * HALO, width), F32),
-            pltpu.VMEM((2, rows + 16, half), BF16),
-            pltpu.VMEM((2, rows + 16, half), BF16),
-            pltpu.VMEM((2, rows + 16, 2 * TILE), F32),
-            pltpu.VMEM((4, 2, half, 2 * TILE), BF16),
-            pltpu.VMEM((4, 2, half, 2 * TILE), BF16),
-            pltpu.VMEM((4, rows, 4 * TILE), F32),
-            pltpu.VMEM((2, rows, 4 * TILE), F32),
-            pltpu.VMEM((rows, 4 * TILE), F32),
-            pltpu.VMEM((freqs, rows, TILE), F32),
-            pltpu.VMEM((freqs, rows, TILE), F32),
-            dma((2, 4)),
+            pltpu.VMEM((2, rows + 16, quarter), BF16),
+            pltpu.VMEM((2, rows + 16, quarter), BF16),
+            pltpu.VMEM((rows + 16, half), BF16),
+            pltpu.VMEM((rows + 16, half), BF16),
+            pltpu.VMEM((2, rows + 16, LANES), F32),
+            pltpu.VMEM((8, 2, 16, LANES), F32),
+            pltpu.VMEM((4, quarter, 256), BF16),
+            pltpu.VMEM((4, quarter, 256), BF16),
+            pltpu.VMEM((4, half, 256), BF16),
+            pltpu.VMEM((4, half, 256), BF16),
+            pltpu.VMEM((8, 256, 512), BF16),
+            pltpu.VMEM((8, 256, 512), BF16),
+            pltpu.VMEM((rows, LANES), BF16),
+            pltpu.VMEM((rows, 256), F32),
+            pltpu.VMEM((2, 4, rows, 256), F32),
+            pltpu.VMEM((2, 2, rows, 256), F32),
+            pltpu.VMEM((2, rows, 256), F32),
+            pltpu.VMEM((2, 4, 8, 4, 8, LANES), F32),
+            pltpu.VMEM((2, 4, 8, 4, 8, LANES), F32),
+            pltpu.VMEM((4, 256, LANES), F32),
+            pltpu.VMEM((2, 4, 256, LANES), F32),
+            pltpu.VMEM((2, 4, 256, LANES), F32),
+            dma((4,)),
+            dma((3, 2, 4)),
             dma((2,)),
             dma((2,)),
-            dma((CHUNKS,)),
-            dma((CHUNKS,)),
-            dma((freqs - 1, CHUNKS)),
-            dma((freqs - 1, CHUNKS)),
+            dma((2, 2, CHUNKS)),
+            dma((2, 2, CHUNKS)),
+            dma((2, CHUNKS)),
+            dma((2, CHUNKS)),
+            dma((2, 3, CHUNKS)),
+            dma((2, 3, CHUNKS)),
+            dma((2, 3)),
+            dma((2, 3)),
         ],
         compiler_params=pltpu.CompilerParams(
             collective_id=0, has_side_effects=True, vmem_limit_bytes=56 * 1024 * 1024
         ),
-        cost_estimate=pl.CostEstimate(flops=7 * 10**9, bytes_accessed=14 * 2**20, transcendentals=0),
-        name="fused",
-    )(info, low, block, high, taps, *tables)
+        cost_estimate=pl.CostEstimate(flops=7 * 10**9, bytes_accessed=18 * 2**20, transcendentals=0),
+        name="joint",
+    )(
+        zero_point, noise_var, footprint.T, accept, assign, stamps, block,
+        joint_tap_table(ids, width, stamp_len),
+        th0, tl0, th1, tl1, cth, ctl, joint_twiddles(), joint_order(ids, width), psf_rows, psf_cols,
+    )
 
 
 def column_tables(height):
@@ -484,6 +786,9 @@
     count_all = assign.shape[0]
     freq_at = lax.axis_index("freq")
     reader_at = lax.axis_index(READERS)
+    sizes = (lax.axis_size("read"), lax.axis_size("pair"), freqs)
+    if sizes == (2, 2, 4) and (rows_dev, width, stamp_len, count_all) == (512, 2048, 16, 4):
+        return joint(exposures[0], stamps, zero_point, noise_var, footprint, accept, assign)
     ids = column_order(width, freqs, readers)
     tiles = ids.shape[1]
     offsets = np.arange(stamp_len) - stamp_len // 2
@@ -512,17 +817,14 @@
     info = jnp.stack([freq_at * rows_dev, low_row, high_row, jnp.int32(height)]).astype(jnp.int32)
 
     tables = row_tables(ids, width)
-    if lax.axis_size("read") == 2 and lax.axis_size("pair") == 2 and tiles == 4 and freqs == 4:
-        gathered = fused(info, low, block, high, taps, tables, freqs)
-    else:
-        terms = front(info, low, block, high, taps, tables)
-        if tiles != readers:
-            terms = terms.reshape(tiles, rows_dev, 2, 2, readers // tiles, TILE * tiles // readers)
-            terms = terms.transpose(0, 4, 1, 2, 3, 5).reshape(readers, rows_dev, -1)
-        summed = lax.psum_scatter(terms, READERS, scatter_dimension=0, tiled=True)
-        summed = summed.reshape(rows_dev, 2, 2, freqs, share // 2)
-        summed = summed.transpose(3, 0, 2, 1, 4).reshape(freqs, rows_dev, 2 * share)
-        gathered = lax.all_to_all(summed, "freq", split_axis=0, concat_axis=0, tiled=True)
+    terms = front(info, low, block, high, taps, tables)
+    if tiles != readers:
+        terms = terms.reshape(tiles, rows_dev, 2, 2, readers // tiles, TILE * tiles // readers)
+        terms = terms.transpose(0, 4, 1, 2, 3, 5).reshape(readers, rows_dev, -1)
+    summed = lax.psum_scatter(terms, READERS, scatter_dimension=0, tiled=True)
+    summed = summed.reshape(rows_dev, 2, 2, freqs, share // 2)
+    summed = summed.transpose(3, 0, 2, 1, 4).reshape(freqs, rows_dev, 2 * share)
+    gathered = lax.all_to_all(summed, "freq", split_axis=0, concat_axis=0, tiled=True)
     grid = columns(gathered.reshape(height, 2 * share), order_matrix(share), column_tables(height))
     grid = lax.all_to_all(
         grid.reshape(readers, out_rows, 2 * share), READERS, split_axis=0, concat_axis=0, tiled=True

time: 106 us -> 65.2 us (0.62); the launches traced: 104 us -> 65 us
  starting transfers between devices: 10.3 us -> 0 us
  waiting for transfers between devices: 10 us -> 0 us
  other arithmetic: 8.97 us -> 0 us
  local copies, waits for them, and re-layouts: 7.49 us -> 2.26 us
  matrix products: 2.16 us -> 0 us
  Pallas kernels: 64.7 us -> 62.7 us
    all_to_all x1 -> x0, waiting for transfers between devices: 10 us -> none  [per_device(): lax.all_to_all(grid.reshape(readers, out_rows, 2 * share), READERS, split...]
    all_to_all x1 -> x0, starting transfers between devices: 6.04 us -> none  [per_device(): lax.all_to_all(grid.reshape(readers, out_rows, 2 * share), READERS, split...]
    ppermute x2 -> x0, starting transfers between devices: 4.27 us -> none  [the longest x1 2.18 us: per_device(): low = lax.ppermute(block[rows_dev - HALO:], 'freq', forward)]
    reduce_sum x3 -> x0, other arithmetic: 4.25 us -> none  [the longest x1 2.12 us: per_device(): low_row = jnp.sum(jnp.where(chosen, footprint[:, 0], 0))]
    dot_general x2 -> x0, matrix products: 2.16 us -> none  [the longest x1 1.16 us: per_device(): taps = jnp.einsum('ab,cbp->cap', stamp, tap_table, precision=HIGHEST)]
    reshape x3 -> x0, local copies, waits for them, and re-layouts: 2.05 us -> none  [the longest x1 1.31 us: per_device(): grid.reshape(readers, out_rows, 2 * share)]
    pallas_call x3 -> x1, Pallas kernels: 64.7 us -> 62.7 us  [joint(): pl.pallas_call(joint_kernel, out_shape=jax.ShapeDtypeStruct((2, rows, 256...]
    div x1 -> x0, other arithmetic: 2.01 us -> none  [per_device(): denom_weight = accepted * zero_point * zero_point / noise_var]
  transfers between devices with their start and end apart: 3 -> 0, of which waited for: 1 -> 0; matrix products, arithmetic and copies ran while one was open for 12% -> 0% of each run, Pallas kernels for 2% -> 0%
where the time goes in v1:
time: 65.2 us; the launch traced here: 65 us
  Pallas kernels  62.7 us (96%)
  local copies, waits for them, and re-layouts  2.26 us (3%)
    pallas_call x1, Pallas kernels, joint(): pl.pallas_call(joint_kernel, out_shape=jax.ShapeDtypeStruct((2, rows, 256...  62.7 us
    unnamed x1, local copies, waits for them, and re-layouts  2.26 us

profile of v1, /device:TPU:1, one launch (start us, length us, event | category | flops | bytes accessed | tf_op | source)
XLA Modules:
  0.0 65.0 jit_solution(5668863683353624489)
XLA Ops:
  0.0 62.7 %joint.1 = f32[2,512,256]{2,1,0:T(8,128)} custom-call(f32[4]{0:T(128)} %zero_point.1, f32[4]{0:T(128)} %noise_var.1, s32[2,4]{1,0:T(2,128)} %bitcast.3, s32[4]{0:T(128)} %accept.1, s32[4]{0:T(128)} %assign.1, f32[4,16,16]{2,1,0:T(8,128)} %stamps.1, f32[512,2048]{1,0:T(8,128)} %bitcast.2, f32[8,16,256]{2,1,0:T(8,128)} %constant.22.clone.tap_table, ...), custom_call_target="tpu_custom_call" | custom-call | flops 7000000000 | bytes 18874368 | tf_op jit(solution)/shard_map/joint/pallas_call | solution.py:637
  62.7 2.3 %copy.20 = f32[2,512,256]{2,1,0:T(8,128)} copy(f32[2,512,256]{2,1,0:T(8,128)} %joint.1) | data formatting | bytes 2097152

commit v2 on v1

--- a/solution.py
+++ b/solution.py
@@ -196,7 +196,8 @@
     for g in range(8):
         phase = angles(np.arange(256), 8 * inner + g, height)
         parts.append(np.concatenate([np.cos(phase), np.sin(phase)], axis=1))
-    return split_np(np.stack(parts))
+    tables = np.stack(split_np(np.stack(parts).reshape(2, 4, 256, 512)))
+    return tables.transpose(2, 0, 1, 3, 4).reshape(4, 1024, 512)
 
 
 def joint_twiddles():
@@ -235,8 +236,8 @@
 def joint_tap_table(ids, width, stamp_len):
     offsets = np.arange(stamp_len) - stamp_len // 2
     phase = [angles(offsets, ids[t], width) for t in range(8)]
-    return np.stack(
-        [np.concatenate([np.cos(x), -np.sin(x)], axis=1) for x in phase]
+    return np.concatenate(
+        [np.concatenate([np.cos(x), -np.sin(x)], axis=1) for x in phase], axis=1
     ).astype(np.float32)
 
 
@@ -256,9 +257,9 @@
 
 def joint_kernel(
     zero_point, noise_var, footprint, accept, assign, stamps, block, tap_table,
-    th0, tl0, th1, tl1, cth, ctl, twiddle, order, psf_rows, psf_cols, out,
-    ext, ch0, cl0, ch1, cl1, grid, taps,
-    bh0, bl0, bh1, bl1, ch_tab, cl_tab, prow, inverse,
+    th0, tl0, th1, tl1, ctab, twiddle, order, psf_rows, psf_cols, out,
+    ext, even, odd, grid, taps,
+    bh0, bl0, bh1, bl1, col_tab, prow, inverse,
     work, pair_in, read_in, freq_out, freq_in, mixed, col_out, col_in,
     block_sem, table_sem, halo_send, halo_recv, pair_send, pair_recv,
     read_send, read_recv, freq_send, freq_recv, col_send, col_recv,
@@ -292,11 +293,8 @@
             for n, (a, b) in enumerate(pairs)
         ]
 
-    def column_table_copies():
-        return (
-            pltpu.make_async_copy(cth, ch_tab, table_sem.at[2, 0, 0]),
-            pltpu.make_async_copy(ctl, cl_tab, table_sem.at[2, 0, 1]),
-        )
+    def column_table_copy():
+        return pltpu.make_async_copy(ctab, col_tab, table_sem.at[2, 0, 0])
 
     def psf_copy():
         return pltpu.make_async_copy(psf_rows.at[me], prow, table_sem.at[2, 0, 2])
@@ -345,8 +343,8 @@
         )
 
     def col_copy(k, n):
-        rd = 1 - r if n > 0 else r
-        pd = p if n == 1 else 1 - p
+        rd = jnp.where(n > 0, 1 - r, r)
+        pd = jnp.where(n == 1, p, 1 - p)
         return pltpu.make_async_remote_copy(
             src_ref=col_out.at[k, 2 * rd + pd], dst_ref=col_in.at[k, me],
             send_sem=col_send.at[k, n], recv_sem=col_recv.at[k, n],
@@ -364,13 +362,9 @@
         )
     for n in range(4):
         block_copy(n).start()
-    for k in range(2):
-        for s in range(4):
-            for copy in row_table_copies(k, s):
-                copy.start()
-    for copy in column_table_copies():
-        copy.start()
-    psf_copy().start()
+    for s in range(2):
+        for copy in row_table_copies(0, s):
+            copy.start()
 
     mine = assign[me]
     first_row = footprint[0, mine]
@@ -379,55 +373,58 @@
     top = accept[mine].astype(F32) * zero_point[mine] * scale
     side = stamps.shape[1]
     stamp = stamps[mine] * (jnp.full((side, side), top, F32) / jnp.full((side, side), noise_var[mine], F32))
+    every = jnp.dot(stamp, tap_table[...], precision=HIGHEST, preferred_element_type=F32)
     for t in range(8):
-        both = jnp.dot(stamp, tap_table[t], precision=HIGHEST, preferred_element_type=F32)
-        taps[t, 0] = both[:, :LANES]
-        taps[t, 1] = both[:, LANES:]
+        for n in range(2):
+            taps[t, n] = every[:, (2 * t + n) * LANES : (2 * t + n + 1) * LANES]
 
     pl.semaphore_wait(barrier, freqs + 2)
     for copy in halo_copies():
         copy.start()
 
-    cols = lax.broadcasted_iota(jnp.int32, (16, width), 1)
-
-    def clean(i, carry):
-        at = pl.multiple_of(i * 16, 16)
+    edge = lax.broadcasted_iota(jnp.int32, (16, LANES), 1)
+    last_lane = width - LANES
+
+    def clean_at(at, rim):
         piece = ext[pl.ds(at, 32), :]
         mid = piece[8:24]
         ids = f * rows - 8 + at + lax.broadcasted_iota(jnp.int32, (16, 1), 0)
-        ids = jnp.where(ids < 0, ids + height, ids)
-        ids = jnp.where(ids >= height, ids - height, ids)
-        up = jnp.where(ids == 0, 0.0, piece[7:23])
-        down = jnp.where(ids == height - 1, 0.0, piece[9:25])
-        left = jnp.where(cols == 0, 0.0, pltpu.roll(mid, 1, 1))
-        right = jnp.where(cols == width - 1, 0.0, pltpu.roll(mid, width - 1, 1))
+        up, down = piece[7:23], piece[9:25]
+        if rim:
+            ids = jnp.where(ids < 0, ids + height, ids)
+            ids = jnp.where(ids >= height, ids - height, ids)
+            up = jnp.where(ids == 0, 0.0, up)
+            down = jnp.where(ids == height - 1, 0.0, down)
+        left = pltpu.roll(mid, 1, 1)
+        left = jnp.concatenate(
+            [jnp.where(edge == 0, 0.0, left[:, :LANES]), left[:, LANES:]], axis=1
+        )
+        right = pltpu.roll(mid, width - 1, 1)
+        right = jnp.concatenate(
+            [right[:, :last_lane], jnp.where(edge == LANES - 1, 0.0, right[:, last_lane:])], axis=1
+        )
         inside = (ids >= first_row) & (ids < last_row)
         cell = jnp.where(inside, mid - 0.25 * (up + down + left + right), 0.0)
         total = cell[:, :half] + cell[:, half:]
         here = pl.ds(at, 16)
-        hi, lo = split(cell[:, :half] - cell[:, half:])
-        ch1[here, :] = hi
-        cl1[here, :] = lo
-        hi, lo = split(total[:, :quarter] + total[:, quarter:])
-        ch0[0, here, :] = hi
-        cl0[0, here, :] = lo
-        hi, lo = split(total[:, :quarter] - total[:, quarter:])
-        ch0[1, here, :] = hi
-        cl0[1, here, :] = lo
-        return carry
+        odd[0, here, :], odd[1, here, :] = split(cell[:, :half] - cell[:, half:])
+        even[0, 0, here, :], even[0, 1, here, :] = split(total[:, :quarter] + total[:, quarter:])
+        even[1, 0, here, :], even[1, 1, here, :] = split(total[:, :quarter] - total[:, quarter:])
 
     for n in range(4):
         block_copy(n).wait()
-    lax.fori_loop(1, rows // 16, clean, 0)
-    for copy in halo_copies():
-        copy.wait_recv()
-    clean(0, 0)
-    clean(rows // 16, 0)
+    for s in range(2, 4):
+        for copy in row_table_copies(0, s):
+            copy.start()
+    for s in range(4):
+        for copy in row_table_copies(1, s):
+            copy.start()
+    column_table_copy().start()
+    psf_copy().start()
 
     lanes = lax.broadcasted_iota(jnp.int32, (32, LANES), 1)
 
     def pack(k, c):
-        read_copy(k, c).wait_recv()
         pair_copy(k, 1, c).wait_recv()
 
         def body(n, carry):
@@ -445,63 +442,87 @@
         for d in range(1, freqs):
             freq_copy(k, d, c).start()
 
-    def groups(k):
-        def step(s, carry):
-            for copy in row_table_copies(k, s):
-                copy.wait()
-            t = group_at(s)
-            if k == 0:
-                xh, xl, wh, wl = ch0[t % 2], cl0[t % 2], bh0[s], bl0[s]
-            else:
-                xh, xl, wh, wl = ch1[...], cl1[...], bh1[s], bl1[s]
-            both = dot(xh, wh) + dot(xh, wl) + dot(xl, wh)
-            grid[0] = both[:, :LANES]
-            grid[1] = both[:, LANES:]
-
-            def fir(c, inner):
-                for n in range(2):
-                    at = pl.multiple_of(c * chunk + n * 64, 64)
-                    sums = [[jnp.zeros((8, LANES), F32), jnp.zeros((8, LANES), F32)] for _ in range(8)]
-                    for a in range(16):
-                        qr = taps[4 * k + t, 0, a : a + 1, :]
-                        qi = taps[4 * k + t, 1, a : a + 1, :]
-                        for g in range(8):
-                            here = pl.ds(at + g + a, 8, stride=8)
-                            xr = grid[0, here, :]
-                            xi = grid[1, here, :]
-                            sums[g][0] = sums[g][0] + (qr * xr + qi * xi)
-                            sums[g][1] = sums[g][1] + (qr * xi - qi * xr)
-                    for g in range(8):
-                        work[k, s, pl.ds(at + 8 * g, 8), :LANES] = sums[g][0]
-                        work[k, s, pl.ds(at + 8 * g, 8), LANES:] = sums[g][1]
-
-                @pl.when(s == 0)
+    def wait_tables(k, s):
+        for copy in row_table_copies(k, s):
+            copy.wait()
+
+    def store_grid(xh, xl, wh, wl):
+        both = dot(xh, wh) + dot(xh, wl) + dot(xl, wh)
+        grid[0] = both[:, :LANES]
+        grid[1] = both[:, LANES:]
+
+    def multiply(k, s):
+        @pl.when(k == 0)
+        def _():
+            wait_tables(0, s)
+            kind = group_at(s) % 2
+            store_grid(even[kind, 0], even[kind, 1], bh0[s], bl0[s])
+
+        @pl.when(k == 1)
+        def _():
+            wait_tables(1, s)
+            store_grid(odd[0], odd[1], bh1[s], bl1[s])
+
+    def fir(k, s, c):
+        t = 4 * k + group_at(s)
+        for n in range(2):
+            at = pl.multiple_of(c * chunk + n * 64, 64)
+            sums = [[jnp.zeros((8, LANES), F32), jnp.zeros((8, LANES), F32)] for _ in range(8)]
+            for a in range(16):
+                qr = taps[t, 0, a : a + 1, :]
+                qi = taps[t, 1, a : a + 1, :]
+                for g in range(8):
+                    here = pl.ds(at + g + a, 8, stride=8)
+                    xr = grid[0, here, :]
+                    xi = grid[1, here, :]
+                    sums[g][0] = sums[g][0] + (qr * xr + qi * xi)
+                    sums[g][1] = sums[g][1] + (qr * xi - qi * xr)
+            for g in range(8):
+                work[k, s, pl.ds(at + 8 * g, 8), :LANES] = sums[g][0]
+                work[k, s, pl.ds(at + 8 * g, 8), LANES:] = sums[g][1]
+
+    def sum_pair(k, c):
+        pair_copy(k, 0, c).wait_recv()
+        part = pl.ds(pl.multiple_of(c * chunk, chunk), chunk)
+        work[k, 1, part, :] = work[k, 1, part, :] + pair_in[k, 0, part, :]
+
+    def group(n, carry):
+        k, s = n // 4, n % 4
+        multiply(k, s)
+
+        def body(c, inner):
+            fir(k, s, c)
+
+            @pl.when(s % 2 == 0)
+            def _():
+                pair_copy(k, s // 2, c).start()
+
+            @pl.when(s == 1)
+            def _():
+                sum_pair(k, c)
+
+                @pl.when(c < 2)
                 def _():
-                    pair_copy(k, 0, c).start()
-
-                @pl.when(s == 2)
-                def _():
-                    pair_copy(k, 1, c).start()
-
-                @pl.when(s == 1)
-                def _():
-                    pair_copy(k, 0, c).wait_recv()
-                    part = pl.ds(pl.multiple_of(c * chunk, chunk), chunk)
-                    work[k, 1, part, :] = work[k, 1, part, :] + pair_in[k, 0, part, :]
                     read_copy(k, c).start()
 
-                return inner
-
-            lax.fori_loop(0, CHUNKS, fir, 0)
-            if k == 1:
-
-                @pl.when(s < 3)
-                def _():
-                    pack(0, s + 1)
-
-            return carry
-
-        lax.fori_loop(0, 4, step, 0)
+            return inner
+
+        lax.fori_loop(0, CHUNKS, body, 0)
+
+        @pl.when(n == 2)
+        def _():
+            read_copy(0, 2).wait_recv()
+            read_copy(0, 0).start()
+
+        @pl.when((n == 5) | (n == 6))
+        def _():
+            read_copy(0, lax.rem(n + 2, 4)).wait_recv()
+
+        @pl.when((n > 2) & (n < 7))
+        def _():
+            pack(0, lax.rem(n + 2, 4))
+
+        return carry
 
     def times_j(x, at):
         real = at % 64 < 32
@@ -512,17 +533,17 @@
             for c in range(CHUNKS):
                 freq_copy(k, d, c).wait_recv()
         freq_in[k, f] = freq_out[k, f]
-        wide = lax.broadcasted_iota(jnp.int32, (256, LANES), 1)
-
-        def body(gg, carry):
+        tall = lax.broadcasted_iota(jnp.int32, (256, LANES), 1)
+
+        def residue(gg, carry):
             x = freq_in[k, :, :, gg].reshape(256, LANES)
-            hi, lo = split(jnp.concatenate([x, times_j(x, wide)], axis=0))
-            rhs = jnp.concatenate([hi, lo], axis=1)
-            sides = []
-            for g in (gg, gg + 4):
-                res = dot(ch_tab[g], rhs)
-                sides.append(res[:, :LANES] + res[:, LANES:] + dot(cl_tab[g], hi))
-            both = jnp.where(wide < 64, sides[0], sides[1])
+            hi, lo = split(jnp.concatenate([x, times_j(x, tall)], axis=0))
+            res = dot(col_tab[gg], jnp.concatenate([hi, lo], axis=1))
+            sides = [
+                res[n : n + 256, :LANES] + res[n : n + 256, LANES:] + res[n + 512 : n + 768, :LANES]
+                for n in (0, 256)
+            ]
+            both = jnp.where(tall < 64, sides[0], sides[1])
             both = pltpu.roll(both, 64, 1) + both * twiddle[gg, 3:4, :]
             mixed[gg] = (
                 both * twiddle[gg, 0:1, :]
@@ -531,7 +552,7 @@
             )
             return carry
 
-        lax.fori_loop(0, 4, body, 0)
+        lax.fori_loop(0, 4, residue, 0)
 
         def last(i, carry):
             here = pl.ds(pl.multiple_of(i * 32, 32), 32)
@@ -567,25 +588,109 @@
                 total = total + weights[e] * (re * re + im * im)
             inverse[here, :] = lax.rsqrt(total)
 
-    groups(0)
-    pack(0, 0)
-    groups(1)
-    denominator()
-    for copy in column_table_copies():
-        copy.wait()
-    columns(0)
-    col_copy(0, 0).start()
-
-    def rest(c, carry):
+    def open_half(i, carry):
+        c0 = 1 + 2 * i
+
+        def piece(t, inner):
+            at = jnp.where(i == 0, 8 + t, jnp.where(t < 7, 25 + t, t - 6))
+            clean_at(pl.multiple_of(at * 16, 16), False)
+            return inner
+
+        lax.fori_loop(0, 17 - 3 * i, piece, 0)
+
+        @pl.when(i == 1)
+        def _():
+            for copy in halo_copies():
+                copy.wait_recv()
+
+            def rim(t, inner):
+                clean_at(pl.multiple_of(t * rows, rows), True)
+                return inner
+
+            lax.fori_loop(0, 2, rim, 0)
+
+        def two(s, inner):
+            @pl.when(i == 0)
+            def _():
+                wait_tables(0, s)
+
+            kind = group_at(s) % 2
+            spots = [
+                pl.ds(pl.multiple_of(lax.rem(c0 + n, CHUNKS) * chunk, chunk), chunk + 16)
+                for n in range(2)
+            ]
+            xh = jnp.concatenate([even[kind, 0, here, :] for here in spots], axis=0)
+            xl = jnp.concatenate([even[kind, 1, here, :] for here in spots], axis=0)
+            both = dot(xh, bh0[s]) + dot(xh, bl0[s]) + dot(xl, bh0[s])
+            for n, here in enumerate(spots):
+                part = both[n * (chunk + 16) : (n + 1) * (chunk + 16)]
+                grid[0, here, :] = part[:, :LANES]
+                grid[1, here, :] = part[:, LANES:]
+
+            def body(n, inner2):
+                c = lax.rem(c0 + n, CHUNKS)
+                fir(0, s, c)
+
+                @pl.when(s == 0)
+                def _():
+                    pair_copy(0, 0, c).start()
+
+                @pl.when(s == 1)
+                def _():
+                    sum_pair(0, c)
+
+                    @pl.when(i == 0)
+                    def _():
+                        read_copy(0, c).start()
+
+                return inner2
+
+            lax.fori_loop(0, 2, body, 0)
+            return inner
+
+        lax.fori_loop(0, 2, two, 0)
+        return carry
+
+    lax.fori_loop(0, 2, open_half, 0)
+    read_copy(0, 1).wait_recv()
+    read_copy(0, 3).start()
+    lax.fori_loop(2, 8, group, 0)
+
+    def receive(c, carry):
+        read_copy(1, c).wait_recv()
+
+        @pl.when(c < 2)
+        def _():
+            read_copy(1, c + 2).start()
+
+        @pl.when(c == 3)
+        def _():
+            col_copy(0, 1).start()
+            col_copy(0, 2).start()
+
         pack(1, c)
         return carry
 
-    lax.fori_loop(0, CHUNKS, rest, 0)
-    col_copy(0, 1).start()
-    col_copy(0, 2).start()
-    columns(1)
-    for n in range(3):
-        col_copy(1, n).start()
+    column_table_copy().wait()
+
+    def ending(k, carry):
+        lax.fori_loop(2 * k, 2 * k + 2, receive, 0)
+
+        @pl.when(k == 1)
+        def _():
+            denominator()
+
+        columns(k)
+        col_copy(k, 0).start()
+
+        @pl.when(k == 1)
+        def _():
+            col_copy(1, 1).start()
+            col_copy(1, 2).start()
+
+        return carry
+
+    lax.fori_loop(0, 2, ending, 0)
     for k in range(2):
         col_in[k, me] = col_out[k, me]
         for n in range(3):
@@ -627,11 +732,10 @@
     stamp_len = stamps.shape[1]
     ids = joint_columns(width)
     th0, tl0, th1, tl1 = joint_row_tables(ids, width)
-    cth, ctl = joint_column_tables(height)
     psf_rows, psf_cols = joint_psf_tables(height, width, stamp_len)
     vmem = pl.BlockSpec(memory_space=pltpu.VMEM)
     smem = pl.BlockSpec(memory_space=pltpu.SMEM)
-    anywhere = pl.BlockSpec(memory_space=pl.ANY)
+    anywhere = pl.BlockSpec(memory_space=pltpu.HBM)
     dma = pltpu.SemaphoreType.DMA
     half, quarter = width // 2, width // 4
     return pl.pallas_call(
@@ -639,23 +743,20 @@
         out_shape=jax.ShapeDtypeStruct((2, rows, 256), F32),
         in_specs=[smem] * 5
         + [vmem, anywhere, vmem]
-        + [anywhere] * 6
+        + [anywhere] * 5
         + [vmem, vmem, anywhere, vmem],
         out_specs=vmem,
         scratch_shapes=[
             pltpu.VMEM((rows + 2 * HALO, width), F32),
-            pltpu.VMEM((2, rows + 16, quarter), BF16),
-            pltpu.VMEM((2, rows + 16, quarter), BF16),
-            pltpu.VMEM((rows + 16, half), BF16),
-            pltpu.VMEM((rows + 16, half), BF16),
+            pltpu.VMEM((2, 2, rows + 16, quarter), BF16),
+            pltpu.VMEM((2, rows + 16, half), BF16),
             pltpu.VMEM((2, rows + 16, LANES), F32),
             pltpu.VMEM((8, 2, 16, LANES), F32),
             pltpu.VMEM((4, quarter, 256), BF16),
             pltpu.VMEM((4, quarter, 256), BF16),
             pltpu.VMEM((4, half, 256), BF16),
             pltpu.VMEM((4, half, 256), BF16),
-            pltpu.VMEM((8, 256, 512), BF16),
-            pltpu.VMEM((8, 256, 512), BF16),
+            pltpu.VMEM((4, 1024, 512), BF16),
             pltpu.VMEM((rows, LANES), BF16),
             pltpu.VMEM((rows, 256), F32),
             pltpu.VMEM((2, 4, rows, 256), F32),
@@ -687,7 +788,7 @@
     )(
         zero_point, noise_var, footprint.T, accept, assign, stamps, block,
         joint_tap_table(ids, width, stamp_len),
-        th0, tl0, th1, tl1, cth, ctl, joint_twiddles(), joint_order(ids, width), psf_rows, psf_cols,
+        th0, tl0, th1, tl1, joint_column_tables(height), joint_twiddles(), joint_order(ids, width), psf_rows, psf_cols,
     )
 
 

time: 65.2 us -> 61.1 us (0.937)
  Pallas kernels: 62.7 us -> 58.7 us
    pallas_call x1, Pallas kernels: 62.7 us -> 58.7 us  [joint(): pl.pallas_call(joint_kernel, out_shape=jax.ShapeDtypeStruct((2, rows, 256...]
where the time goes in v2:
time: 61.1 us; the launch traced here: 60.9 us
  Pallas kernels  58.7 us (96%)
  local copies, waits for them, and re-layouts  2.26 us (4%)
    pallas_call x1, Pallas kernels, joint(): pl.pallas_call(joint_kernel, out_shape=jax.ShapeDtypeStruct((2, rows, 256...  58.7 us
    unnamed x1, local copies, waits for them, and re-layouts  2.26 us

profile of v2, /device:TPU:1, one launch (start us, length us, event | category | flops | bytes accessed | tf_op | source)
XLA Modules:
  0.0 60.9 jit_solution(13410242188052213887)
XLA Ops:
  0.0 58.7 %joint.1 = f32[2,512,256]{2,1,0:T(8,128)} custom-call(f32[4]{0:T(128)} %zero_point.1, f32[4]{0:T(128)} %noise_var.1, s32[2,4]{1,0:T(2,128)} %bitcast.3, s32[4]{0:T(128)} %accept.1, s32[4]{0:T(128)} %assign.1, f32[4,16,16]{2,1,0:T(8,128)} %stamps.1, f32[512,2048]{1,0:T(8,128)} %bitcast.2, f32[16,2048]{1,0:T(8,128)} %constant.20.clone.tap_table, ...), custom_call_target="tpu_custom_call" | custom-call | flops 7000000000 | bytes 18874368 | tf_op jit(solution)/shard_map/joint/pallas_call | solution.py:741
  58.7 2.3 %copy.19 = f32[2,512,256]{2,1,0:T(8,128)} copy(f32[2,512,256]{2,1,0:T(8,128)} %joint.1) | data formatting | bytes 2097152

commit v3 on v2

--- a/solution.py
+++ b/solution.py
@@ -518,6 +518,10 @@
         def _():
             read_copy(0, lax.rem(n + 2, 4)).wait_recv()
 
+        @pl.when((n == 5) | (n == 6))
+        def _():
+            read_copy(1, n - 3).start()
+
         @pl.when((n > 2) & (n < 7))
         def _():
             pack(0, lax.rem(n + 2, 4))
@@ -552,7 +556,7 @@
             )
             return carry
 
-        lax.fori_loop(0, 4, residue, 0)
+        lax.fori_loop(0, 4, residue, 0, unroll=True)
 
         def last(i, carry):
             here = pl.ds(pl.multiple_of(i * 32, 32), 32)
@@ -565,7 +569,7 @@
             col_out[k, 3, here, :] = c - d
             return carry
 
-        lax.fori_loop(0, 8, last, 0)
+        lax.fori_loop(0, 8, last, 0, unroll=2)
 
     def denominator():
         psf_copy().wait()
@@ -659,10 +663,6 @@
     def receive(c, carry):
         read_copy(1, c).wait_recv()
 
-        @pl.when(c < 2)
-        def _():
-            read_copy(1, c + 2).start()
-
         @pl.when(c == 3)
         def _():
             col_copy(0, 1).start()
@@ -674,7 +674,7 @@
     column_table_copy().wait()
 
     def ending(k, carry):
-        lax.fori_loop(2 * k, 2 * k + 2, receive, 0)
+        lax.fori_loop(3 * k, 3 + k, receive, 0)
 
         @pl.when(k == 1)
         def _():
@@ -711,7 +711,7 @@
             out[q % 2, here, :] = result[64 * q : 64 * (q + 1)] * inverse[here, :]
         return carry
 
-    lax.fori_loop(0, 4, finish, 0)
+    lax.fori_loop(0, 4, finish, 0, unroll=True)
 
     for copy in halo_copies():
         copy.wait_send()

time: 61.1 us -> 59 us (0.966)
  Pallas kernels: 58.7 us -> 56.6 us
    pallas_call x1, Pallas kernels: 58.7 us -> 56.6 us  [joint(): pl.pallas_call(joint_kernel, out_shape=jax.ShapeDtypeStruct((2, rows, 256...]
where the time goes in v3:
time: 59 us; the launch traced here: 58.9 us
  Pallas kernels  56.6 us (96%)
  local copies, waits for them, and re-layouts  2.26 us (4%)
    pallas_call x1, Pallas kernels, joint(): pl.pallas_call(joint_kernel, out_shape=jax.ShapeDtypeStruct((2, rows, 256...  56.6 us
    unnamed x1, local copies, waits for them, and re-layouts  2.26 us

profile of v3, /device:TPU:1, one launch (start us, length us, event | category | flops | bytes accessed | tf_op | source)
XLA Modules:
  0.0 58.9 jit_solution(16503850630880687267)
XLA Ops:
  0.0 56.6 %joint.1 = f32[2,512,256]{2,1,0:T(8,128)} custom-call(f32[4]{0:T(128)} %zero_point.1, f32[4]{0:T(128)} %noise_var.1, s32[2,4]{1,0:T(2,128)} %bitcast.3, s32[4]{0:T(128)} %accept.1, s32[4]{0:T(128)} %assign.1, f32[4,16,16]{2,1,0:T(8,128)} %stamps.1, f32[512,2048]{1,0:T(8,128)} %bitcast.2, f32[16,2048]{1,0:T(8,128)} %constant.20.clone.tap_table, ...), custom_call_target="tpu_custom_call" | custom-call | flops 7000000000 | bytes 18874368 | tf_op jit(solution)/shard_map/joint/pallas_call | solution.py:741
  56.6 2.3 %copy.19 = f32[2,512,256]{2,1,0:T(8,128)} copy(f32[2,512,256]{2,1,0:T(8,128)} %joint.1) | data formatting | bytes 2097152

commit v4 on v3

--- a/solution.py
+++ b/solution.py
@@ -691,27 +691,28 @@
         return carry
 
     lax.fori_loop(0, 2, ending, 0)
+    wide = lax.broadcasted_iota(jnp.int32, (64, LANES), 1)
     for k in range(2):
         col_in[k, me] = col_out[k, me]
         for n in range(3):
             col_copy(k, n).wait_recv()
-
-    wide = lax.broadcasted_iota(jnp.int32, (64, LANES), 1)
-
-    def finish(i, carry):
-        at = pl.multiple_of(i * 64, 64)
-        parts = []
-        for k in range(2):
+        place = order[k * LANES : (k + 1) * LANES, :]
+
+        def finish(i, carry, k=k, place=place):
+            at = pl.multiple_of(i * 64, 64)
             quads = [col_in[k, n, pl.ds(at, 64), :] for n in range(4)]
-            parts.append(jnp.concatenate(turn(quads, wide), axis=0))
-        hi, lo = split(jnp.concatenate(parts, axis=1))
-        result = dot(hi, order[...]) + dot(lo, order[...])
-        for q in range(4):
-            here = pl.ds(256 * (q // 2) + at, 64)
-            out[q % 2, here, :] = result[64 * q : 64 * (q + 1)] * inverse[here, :]
-        return carry
-
-    lax.fori_loop(0, 4, finish, 0, unroll=True)
+            hi, lo = split(jnp.concatenate(turn(quads, wide), axis=0))
+            result = dot(hi, place) + dot(lo, place)
+            for q in range(4):
+                here = pl.ds(256 * (q // 2) + at, 64)
+                value = result[64 * q : 64 * (q + 1)]
+                if k == 0:
+                    out[q % 2, here, :] = value
+                else:
+                    out[q % 2, here, :] = (out[q % 2, here, :] + value) * inverse[here, :]
+            return carry
+
+        lax.fori_loop(0, 4, finish, 0, unroll=True)
 
     for copy in halo_copies():
         copy.wait_send()

time: 59 us -> 58.8 us (level)
  no operation moved by 1% of the time
where the time goes in v4:
time: 58.8 us; the launch traced here: 58.6 us
  Pallas kernels  56.4 us (96%)
  local copies, waits for them, and re-layouts  2.26 us (4%)
    pallas_call x1, Pallas kernels, joint(): pl.pallas_call(joint_kernel, out_shape=jax.ShapeDtypeStruct((2, rows, 256...  56.4 us
    unnamed x1, local copies, waits for them, and re-layouts  2.26 us

profile of v4, /device:TPU:1, one launch (start us, length us, event | category | flops | bytes accessed | tf_op | source)
XLA Modules:
  0.0 58.6 jit_solution(13212292787363000387)
XLA Ops:
  0.0 56.4 %joint.1 = f32[2,512,256]{2,1,0:T(8,128)} custom-call(f32[4]{0:T(128)} %zero_point.1, f32[4]{0:T(128)} %noise_var.1, s32[2,4]{1,0:T(2,128)} %bitcast.3, s32[4]{0:T(128)} %accept.1, s32[4]{0:T(128)} %assign.1, f32[4,16,16]{2,1,0:T(8,128)} %stamps.1, f32[512,2048]{1,0:T(8,128)} %bitcast.2, f32[16,2048]{1,0:T(8,128)} %constant.20.clone.tap_table, ...), custom_call_target="tpu_custom_call" | custom-call | flops 7000000000 | bytes 18874368 | tf_op jit(solution)/shard_map/joint/pallas_call | solution.py:742
  56.4 2.3 %copy.19 = f32[2,512,256]{2,1,0:T(8,128)} copy(f32[2,512,256]{2,1,0:T(8,128)} %joint.1) | data formatting | bytes 2097152

commit v5 on v4

--- a/solution.py
+++ b/solution.py
@@ -438,7 +438,7 @@
                 freq_out[k, to, b] = value.reshape(4, 8, LANES)
             return carry
 
-        lax.fori_loop(0, 2, body, 0)
+        lax.fori_loop(0, 2, body, 0, unroll=True)
         for d in range(1, freqs):
             freq_copy(k, d, c).start()
 
@@ -569,7 +569,7 @@
             col_out[k, 3, here, :] = c - d
             return carry
 
-        lax.fori_loop(0, 8, last, 0, unroll=2)
+        lax.fori_loop(0, 8, last, 0, unroll=True)
 
     def denominator():
         psf_copy().wait()

time: 58.8 us -> 58.7 us (level)
  no operation moved by 1% of the time
where the time goes in v5:
time: 58.7 us; the launch traced here: 58.5 us
  Pallas kernels  56.3 us (96%)
  local copies, waits for them, and re-layouts  2.26 us (4%)
    pallas_call x1, Pallas kernels, joint(): pl.pallas_call(joint_kernel, out_shape=jax.ShapeDtypeStruct((2, rows, 256...  56.3 us
    unnamed x1, local copies, waits for them, and re-layouts  2.26 us

profile of v5, /device:TPU:1, one launch (start us, length us, event | category | flops | bytes accessed | tf_op | source)
XLA Modules:
  0.0 58.5 jit_solution(9885810365184182995)
XLA Ops:
  0.0 56.3 %joint.1 = f32[2,512,256]{2,1,0:T(8,128)} custom-call(f32[4]{0:T(128)} %zero_point.1, f32[4]{0:T(128)} %noise_var.1, s32[2,4]{1,0:T(2,128)} %bitcast.3, s32[4]{0:T(128)} %accept.1, s32[4]{0:T(128)} %assign.1, f32[4,16,16]{2,1,0:T(8,128)} %stamps.1, f32[512,2048]{1,0:T(8,128)} %bitcast.2, f32[16,2048]{1,0:T(8,128)} %constant.20.clone.tap_table, ...), custom_call_target="tpu_custom_call" | custom-call | flops 7000000000 | bytes 18874368 | tf_op jit(solution)/shard_map/joint/pallas_call | solution.py:742
  56.3 2.3 %copy.19 = f32[2,512,256]{2,1,0:T(8,128)} copy(f32[2,512,256]{2,1,0:T(8,128)} %joint.1) | data formatting | bytes 2097152
